TPU v7x, 32 devices: a whole 2x2x4 slice. The times are simulated.
32 devices in a mesh: row: 4 (over y, x), lmk: 4 (over z), bw: 2 (over core).
Axes of the slice: x: 2, y: 2, z: 4, core: 2. Of those that a mesh axis runs over, the one named last changes fastest.
Arguments:
- embeddings: bfloat16 [6144, 1024], P(('row', 'lmk')), may hold values from -6 to 6
- candidates: bfloat16 [32768, 1024], P(('row', 'lmk')), may hold values from -6 to 6
- block_owner: int32 [2], replicated, may hold values from 0 to 15, as said below
- landmark_picks: int32 [2, 2048], replicated, may hold values from 0 to 2047, each once within a row
- inverse_width: float32 [8], P('bw'), may hold values from 2 to 16
- mixture: float32 [8], P('bw'), may hold values from 0.05 to 0.25
- whitening: bfloat16 [4096, 4096], P(None, 'bw'), may hold values from -0.09375 to 0.09375
Outputs:
- features: bfloat16 [6144, 4096], P(('row', 'lmk'), 'bw')
Inputs may be any that keep to these rules, and one draw needn't show every extreme that they name: `block_owner`: the 2 owners are different, and 15 is one of them. `landmark_picks`: each row is an ordering of 0 to 2047.
All inputs are finite; a program needn't handle non-finite values.
Results may differ from a plain program's by a relative error of at most 0.0055.
Values may be sent and summed in bfloat16 or wider, within the bound.
A program may use at most 128 MiB of HBM per device.

v0:
```python
import jax
import jax.numpy as jnp
from jax import lax
from jax.sharding import PartitionSpec as P


def spread(block, axis, source):
    block = jnp.where(lax.axis_index(axis) == source, block, jnp.zeros_like(block))
    return lax.psum(block, axis)


def normalize(matrix_rows):
    widened = matrix_rows.astype(jnp.float32)
    scale = lax.rsqrt(jnp.sum(widened * widened, axis=-1, keepdims=True) + 1e-06)
    return (widened * scale).astype(jnp.bfloat16)


def kernel_of(cosine, widths, weights):
    running = jnp.zeros(cosine.shape, jnp.float32)
    for which in range(widths.shape[0]):
        running = running + weights[which] * jnp.exp(2.0 * widths[which] * cosine)
    return running


def inner_products(unit_rows, landmark):
    return jnp.einsum("rd,md->rm", unit_rows, landmark, preferred_element_type=jnp.float32)


def per_device(
    embeddings, candidates, block_owner, landmark_picks, inverse_width, mixture, whitening
):
    unit_rows = normalize(embeddings)
    block_count = block_owner.shape[0]
    landmark_blocks = []
    for number in range(block_count):
        owner = block_owner[number]
        chosen = jnp.take(candidates, landmark_picks[number], axis=0)
        arrived = spread(chosen, ("row", "lmk"), owner)
        landmark_blocks.append(normalize(arrived))
    partial_value = jnp.concatenate(
        [
            kernel_of(inner_products(unit_rows, landmark), inverse_width, mixture)
            for landmark in landmark_blocks
        ],
        axis=1,
    )
    kernel = lax.psum(partial_value, "bw").astype(jnp.bfloat16)
    features = jnp.dot(kernel, whitening, preferred_element_type=jnp.float32)
    return features.astype(jnp.bfloat16)


def solution(mesh):
    in_specs = (
        P(("row", "lmk"), None),
        P(("row", "lmk"), None),
        P(),
        P(),
        P("bw"),
        P("bw"),
        P(None, "bw"),
    )
    out_specs = P(("row", "lmk"), "bw")
    return jax.shard_map(
        per_device, mesh=mesh, in_specs=in_specs, out_specs=out_specs, check_vma=False
    )
```

profile of v0, /device:TPU:0, one launch (start us, length us, event | category | flops | bytes accessed | tf_op | source)
XLA Modules:
  0.0 365.1 jit_solution(14540401020606714814)
XLA Ops:
  6.5 0.0 all-reduce.4.cloned.1.call-start
  6.5 0.8 fusion.25
  7.4 1.3 fusion.28
  10.0 13.7 %gather_fusion = bf16[2048,1024]{1,0:T(8,128)(2,1)} fusion(bf16[2048,1024]{1,0:T(8,128)(2,1)} %param.10, s32[2048]{0:T(1024)S(1)} %fusion.23), kind=kCustom, calls=%fused_computation.clone | custom fusion | bytes 8396800 | tf_op jit(solution)/shard_map/jit(_take)/gather | solution.py:37
  23.8 13.7 %gather_fusion.1 = bf16[2048,1024]{1,0:T(8,128)(2,1)} fusion(bf16[2048,1024]{1,0:T(8,128)(2,1)} %param.10, s32[2048]{0:T(1024)S(1)} %fusion.24), kind=kCustom, calls=%fused_computation.1.clone | custom fusion | bytes 8396800 | tf_op jit(solution)/shard_map/jit(_take)/gather | solution.py:37
  37.5 0.0 copy-start
  37.5 4.0 %select_select_fusion.1 = bf16[2048,1024]{1,0:T(8,128)(2,1)} fusion(bf16[2048,1024]{1,0:T(8,128)(2,1)} %gather_fusion, pred[2048]{0:T(1024)(128)(4,1)S(1)} %compare_and_fusion.1, pred[]{:T(512)S(6)} %eq.6), kind=kLoop, calls=%fused_computation.14 | loop fusion | flops 4194304 | bytes 8390657 | tf_op jit(solution)/shard_map/jit(_where)/select_n | solution.py:8
  41.5 0.5 copy-done
  42.0 2.3 select_select_fusion
  44.3 0.0 copy-start.4
  44.3 0.0 copy-start.5
  44.3 0.0 copy-start.3
  44.3 0.0 all-reduce.4.cloned.1.call-update
  44.3 0.6 copy-done.4
  45.0 0.7 fusion.27
  48.2 0.0 copy-done.5
  48.2 0.7 fusion.26
  48.9 0.0 copy-done.3
  48.9 0.2 fusion.19
  49.1 256.1 %all-reduce.4.cloned.1.call-done = (bf16[2048,1024]{1,0:T(8,128)(2,1)}, bf16[2048,1024]{1,0:T(8,128)(2,1)}) async-done(((bf16[2048,1024]{1,0:T(8,128)(2,1)}, bf16[2048,1024]{1,0:T(8,128)(2,1)}), (bf16[2048,1024]{1,0:T(8,128)(2,1)}, bf16[2048,1024]{1,0:T(8,128)(2,1)})) %all-reduce.4.cloned.1.call-update) | async-done | bytes 8388624 | tf_op jit(solution)/shard_map/psum | solution.py:9
  305.2 0.0 copy-start.2
  305.2 5.3 %fusion = (f32[2048]{0:T(1024)S(1)}, f32[2048]{0:T(1024)S(1)}) fusion(bf16[2048,1024]{1,0:T(8,128)(2,1)} %get-tuple-element.7, bf16[2048,1024]{1,0:T(8,128)(2,1)} %get-tuple-element.6), kind=kLoop, calls=%fused_computation.6 | loop fusion | flops 12578816 | bytes 8404992 | tf_op jit(solution)/shard_map/reduce_sum | solution.py:14
  310.5 0.0 copy-done.2
  310.6 0.0 copy-start.1
  310.6 6.5 %multiply_add_fusion.1 = f32[384,2048]{1,0:T(8,128)S(1)} fusion(bf16[2048,1024]{1,0:T(8,128)(2,1)S(1)} %copy-done.2, f32[2048]{0:T(1024)S(1)} %add_rsqrt_fusion.1, f32[]{:T(128)} %bitcast.9, f32[]{:T(128)} %bitcast.8, f32[]{:T(128)} %bitcast.7, f32[]{:T(128)} %bitcast.6, f32[]{:T(128)} %bitcast.5, f32[]{:T(128)} %bitcast.4, f32[]{:T(128)} %bitcast.1, ...), kind=kOutput, calls=%fused_computation.20 | convolution fusion | flops 1626734592 | bytes 8136224 | tf_op jit(solution)/shard_map/rd,md->rm/dot_general | solution.py:26
  317.0 0.0 copy-done.1
  317.0 6.2 %multiply_add_fusion = f32[384,2048]{1,0:T(8,128)S(1)} fusion(bf16[2048,1024]{1,0:T(8,128)(2,1)S(1)} %copy-done.1, f32[2048]{0:T(1024)S(1)} %add_rsqrt_fusion, f32[]{:T(128)} %bitcast.9, f32[]{:T(128)} %bitcast.8, f32[]{:T(128)} %bitcast.7, f32[]{:T(128)} %bitcast.6, f32[]{:T(128)} %bitcast.5, f32[]{:T(128)} %bitcast.4, f32[]{:T(128)} %bitcast.1, ...), kind=kOutput, calls=%fused_computation.19 | convolution fusion | flops 1626734592 | bytes 8136224 | tf_op jit(solution)/shard_map/rd,md->rm/dot_general | solution.py:26
  323.2 3.1 pad_maximum_fusion
  326.3 20.4 %all-reduce.5 = bf16[384,4096]{1,0:T(8,128)(2,1)S(1)} all-reduce(f32[384,4096]{1,0:T(8,128)} %pad_maximum_fusion), channel_id=1, replica_groups=mesh['row'=4,'lmk'=4,'bw'=2] {'bw'}, use_global_device_ids=true, to_apply=%region_5.7 | all-reduce | flops 1572864 | bytes 9437184 | tf_op jit(solution)/shard_map/psum | solution.py:47
  346.7 11.6 %fusion.12 = bf16[384,2048]{1,0:T(8,128)(2,1)} fusion(bf16[4096,2048]{1,0:T(8,128)(2,1)} %param.15, bf16[384,4096]{1,0:T(8,128)(2,1)S(1)} %all-reduce.5), kind=kOutput, calls=%fused_computation.21 | convolution fusion | flops 6443237376 | bytes 21495808 | tf_op jit(solution)/shard_map/dot_general | solution.py:48
  (7 shorter events, 0.0 us)
Async XLA Ops:
  6.5 298.7 %all-reduce.4.cloned.1.call-start = ((), (), s32[]{:S(2)}) async-start(), calls=%async_computation | async-start | bytes 16777216 | tf_op jit(solution)/shard_map/psum | solution.py:9
  37.5 4.6 %copy-start = (bf16[2048,1024]{1,0:T(8,128)(2,1)S(1)}, bf16[2048,1024]{1,0:T(8,128)(2,1)}, u32[]{:S(2)}) copy-start(bf16[2048,1024]{1,0:T(8,128)(2,1)} %gather_fusion.1) | copy-start | bytes 12582916
  44.3 0.7 copy-start.4
  44.3 3.9 %copy-start.5 = (f32[4]{0:T(128)S(1)}, f32[4]{0:T(128)}, u32[]{:S(2)}) copy-start(f32[4]{0:T(128)} %param.14) | copy-start | bytes 52
  44.3 4.6 %copy-start.3 = (bf16[384,1024]{1,0:T(8,128)(2,1)S(1)}, bf16[384,1024]{1,0:T(8,128)(2,1)}, u32[]{:S(2)}) copy-start(bf16[384,1024]{1,0:T(8,128)(2,1)} %param.9) | copy-start | bytes 2359300
  305.2 5.3 %copy-start.2 = (bf16[2048,1024]{1,0:T(8,128)(2,1)S(1)}, bf16[2048,1024]{1,0:T(8,128)(2,1)}, u32[]{:S(2)}) copy-start(bf16[2048,1024]{1,0:T(8,128)(2,1)} %get-tuple-element.7) | copy-start | bytes 12582916
  310.6 6.5 %copy-start.1 = (bf16[2048,1024]{1,0:T(8,128)(2,1)S(1)}, bf16[2048,1024]{1,0:T(8,128)(2,1)}, u32[]{:S(2)}) copy-start(bf16[2048,1024]{1,0:T(8,128)(2,1)} %get-tuple-element.6) | copy-start | bytes 12582916
Sparse Core Ops, SparseCore 0:
  44.5 260.7 all-reduce.3
where the time goes:
time: 366 us; the launch traced here: 365 us
  waiting for transfers between devices  256 us (70%)
  local copies, waits for them, and re-layouts  32.1 us (9%)
  matrix products  24.2 us (7%)
  blocking collectives  20.4 us (6%)
  between operations  17.4 us (5%)
  other arithmetic  14.9 us (4%)
    psum x1, waiting for transfers between devices, spread(): return lax.psum(block, axis)  256 us
    gather x2, local copies, waits for them, and re-layouts, per_device(): chosen = jnp.take(candidates, landmark_picks[number], axis=0)  27.4 us
    psum x1, blocking collectives, per_device(): kernel = lax.psum(partial_value, 'bw').astype(jnp.bfloat16)  20.4 us
    dot_general x2, matrix products, inner_products(): jnp.einsum('rd,md->rm', unit_rows, landmark, preferred_element_type=jnp.f...  12.6 us
    dot_general x1, matrix products, per_device(): features = jnp.dot(kernel, whitening, preferred_element_type=jnp.float32)  11.6 us
  transfers between devices with their start and end apart: 1, of which 1 were waited for; matrix products, arithmetic and copies ran while one was open for 0% of the time, Pallas kernels for 0%

commit v1 on v0

v1 whole, which is shorter than its diff:
```python
import functools
import random

import jax
import jax.numpy as jnp
import numpy as np
from jax import lax
from jax.experimental import pallas as pl
from jax.experimental.pallas import tpu as pltpu
from jax.sharding import PartitionSpec as P

MESH = pl.DeviceIdType.MESH
TREES = 3
STEP_ROWS = 16


class Chips:
    def __init__(self, rows, lmks):
        self.rows, self.lmks = rows, lmks
        self.count = rows * lmks
        self.torus = rows != 4
        if self.torus:
            assert rows == 8 and lmks == 8
            self.back = (1, 0, 3, 2, 5, 4)
        else:
            self.back = (0, 1, 3, 2)
        self.links = len(self.back)

    def neighbour(self, link, row, lmk):
        if not self.torus:
            if link == 0:
                return (row + 2) % 4, lmk
            if link == 1:
                return row + 1 - 2 * (row % 2), lmk
            return row, lmk + (1 if link == 2 else -1)
        x, y, z = row % 4, lmk % 4, (row // 4) * 2 + lmk // 4
        step = 1 if link % 2 == 0 else 3
        if link // 2 == 0:
            x = (x + step) % 4
        elif link // 2 == 1:
            y = (y + step) % 4
        else:
            z = (z + step) % 4
        return (z // 2) * 4 + x, (z % 2) * 4 + y

    def present(self, link, lmk):
        if self.torus or link < 2:
            return None
        return lmk < self.lmks - 1 if link == 2 else lmk > 0

    def degree(self, lmk):
        if self.torus:
            return self.links
        return 2 + jnp.minimum(lmk, 1) + jnp.minimum(self.lmks - 1 - lmk, 1)

    def edges(self, chip):
        row, lmk = chip // self.lmks, chip % self.lmks
        for link in range(self.links):
            here = self.present(link, lmk)
            if here is None or here:
                r, k = self.neighbour(link, row, lmk)
                yield link, r * self.lmks + k


GRID_TREES = [
    [
        [0, 0, 1, 2, 5, 1, 2, 3, 9, 1, 2, 3, 13, 5, 13, 14],
        [0, 9, 10, 11, 12, 13, 14, 15, 0, 8, 9, 10, 8, 9, 10, 11],
        [0, 5, 6, 7, 0, 4, 5, 6, 12, 13, 14, 15, 4, 12, 6, 7],
    ],
    [
        [1, 1, 1, 2, 0, 4, 2, 3, 0, 10, 2, 3, 8, 14, 6, 7],
        [4, 1, 6, 7, 5, 1, 5, 6, 12, 13, 14, 15, 4, 5, 13, 14],
        [8, 1, 10, 11, 12, 13, 14, 15, 9, 1, 9, 10, 13, 9, 10, 11],
    ],
]


def torus_trees(chips):
    for seed in range(1000):
        draw = random.Random(seed)
        used, trees = set(), []
        for tree in range(TREES):
            parent, level = {0: 0}, [0]
            while level:
                following = []
                draw.shuffle(level)
                for chip in level:
                    for link, other in chips.edges(chip):
                        if other in parent or (chip, link) in used:
                            continue
                        if chip == 0 and link // 2 != tree:
                            continue
                        used.add((chip, link))
                        parent[other] = chip
                        following.append(other)
                level = following
            trees.append(parent)
        if all(len(parent) == chips.count for parent in trees):
            return [[parent[chip] for chip in range(chips.count)] for parent in trees]
    raise ValueError("no trees")


def moved(chips, owner):
    if not chips.torus:
        y, x, z = owner // 8, owner // 4 % 2, owner % 4
        turn = z >= 2
        image = [
            ((c // 8) ^ y) * 8 + ((c // 4 % 2) ^ x) * 4 + (3 - c % 4 if turn else c % 4)
            for c in range(16)
        ]
        return image, (3 - z if turn else z)

    def place(chip):
        row, lmk = chip // 8, chip % 8
        return row % 4, lmk % 4, (row // 4) * 2 + lmk // 4

    away = place(owner)
    image = []
    for chip in range(chips.count):
        x, y, z = ((a + b) % 4 for a, b in zip(place(chip), away))
        image.append(((z // 2) * 4 + x) * 8 + (z % 2) * 4 + y)
    return image, 0


@functools.lru_cache(maxsize=None)
def routes(rows, lmks):
    chips = Chips(rows, lmks)
    stored = [torus_trees(chips)] if chips.torus else GRID_TREES
    n = chips.count
    parent_link = np.full((n, n, TREES), -1, np.int32)
    depth = np.zeros((n, n, TREES), np.int32)
    leaving = np.zeros((n, n, chips.links), np.int32)
    for owner in range(n):
        image, root = moved(chips, owner)
        for tree in range(TREES):
            parent = [0] * n
            for chip in range(n):
                parent[image[chip]] = image[stored[root][tree][chip]]
            for chip in range(n):
                if chip == owner:
                    continue
                for link, other in chips.edges(parent[chip]):
                    if other == chip:
                        leaving[owner, parent[chip], link] = tree
                        parent_link[owner, chip, tree] = chips.back[link]
                        break
                at = chip
                while at != owner:
                    at = parent[at]
                    depth[owner, chip, tree] += 1
    return parent_link, depth, leaving


def flood(chips, rounds, parent_ref, leaving_ref, own_ref, land_ref, arrive, leave, send_sem, recv_sem):
    row, lmk = lax.axis_index("row"), lax.axis_index("lmk")
    steps = own_ref.shape[1]
    blocks = land_ref.shape[0]

    def each_link(act):
        for link in range(chips.links):
            here = chips.present(link, lmk)
            if here is None:
                act(link)
            else:
                pl.when(here)(functools.partial(act, link))

    def target(link):
        r, k = chips.neighbour(link, row, lmk)
        return {"row": r, "lmk": k}

    def outgoing(block, slot, link):
        return pltpu.make_async_remote_copy(
            src_ref=leave.at[block, slot, link],
            dst_ref=arrive.at[block, slot, chips.back[link]],
            send_sem=send_sem.at[block, slot, link],
            recv_sem=recv_sem.at[block, slot, chips.back[link]],
            device_id=target(link),
            device_id_type=MESH,
        )

    def incoming(block, slot, link):
        return pltpu.make_async_remote_copy(
            src_ref=leave.at[block, slot, link],
            dst_ref=arrive.at[block, slot, link],
            send_sem=send_sem.at[block, slot, link],
            recv_sem=recv_sem.at[block, slot, link],
            device_id=target(link),
            device_id_type=MESH,
        )

    barrier = pltpu.get_barrier_semaphore()

    def greet(link):
        pl.semaphore_signal(barrier, inc=1, device_id=target(link), device_id_type=MESH)

    each_link(greet)
    pl.semaphore_wait(barrier, chips.degree(lmk))

    def one_round(step, first, last):
        slot, before = step % 2, (step + 1) % 2
        for block in range(blocks):
            if not first:
                each_link(lambda link: incoming(block, before, link).wait_recv())
            held = []
            for tree in range(TREES):
                origin = parent_ref[block, tree]
                value = own_ref[tree, jnp.minimum(step, steps - 1)]
                if not first:
                    for link in range(chips.links):
                        value = lax.select(origin == link, arrive[block, before, link], value)
                land_ref[block, tree, step] = value
                held.append(value)
            if last:
                continue

            def send(link):
                if not first:

                    @pl.when(step >= 2)
                    def _():
                        outgoing(block, slot, link).wait_send()

                tree = leaving_ref[block, link]
                value = lax.select(tree == 1, held[1], held[0])
                leave[block, slot, link] = lax.select(tree == 2, held[2], value)
                outgoing(block, slot, link).start()

            each_link(send)

    one_round(0, True, False)

    def middle(step, carry):
        one_round(step, False, False)
        return carry

    lax.fori_loop(1, rounds - 1, middle, 0)
    one_round(rounds - 1, False, True)
    for block in range(blocks):
        for slot in range(2):
            each_link(lambda link: outgoing(block, slot, link).wait_send())


def normalize(widened):
    scale = lax.rsqrt(jnp.sum(widened * widened, axis=-1, keepdims=True) + 1e-06)
    return (widened * scale).astype(jnp.bfloat16)


def kernel_of(cosine, widths, weights):
    running = jnp.zeros(cosine.shape, jnp.float32)
    for which in range(widths.shape[0]):
        running = running + weights[which] * jnp.exp(2.0 * widths[which] * cosine)
    return running


def per_device(
    chips, embeddings, candidates, block_owner, landmark_picks, inverse_width, mixture, whitening
):
    me = lax.axis_index("row") * chips.lmks + lax.axis_index("lmk")
    core = lax.axis_index("bw")
    blocks, block_rows = landmark_picks.shape
    width = embeddings.shape[1]
    half = block_rows // 2
    steps = -(-half // (TREES * STEP_ROWS))
    parent_link, depth, leaving = routes(chips.rows, chips.lmks)
    deepest = int(depth.max())
    rounds = steps + deepest

    widths = lax.all_gather(inverse_width, "bw", tiled=True)
    weights = lax.all_gather(mixture, "bw", tiled=True)

    picks = jnp.where(block_owner[1] == me, landmark_picks[1], landmark_picks[0])
    picks = lax.dynamic_slice(picks, (core * half,), (half,))
    places = (picks[:, None] == jnp.arange(block_rows, dtype=jnp.int32)[None, :]).astype(jnp.bfloat16)
    chosen = normalize(jnp.dot(places, candidates, preferred_element_type=jnp.float32))
    own = jnp.pad(chosen, ((0, TREES * steps * STEP_ROWS - half), (0, 0)))
    own = own.reshape(TREES, steps, STEP_ROWS, width)

    my_parent = jnp.asarray(parent_link)[block_owner, me]
    my_depth = jnp.asarray(depth)[block_owner, me]
    my_leaving = jnp.asarray(leaving)[block_owner, me]

    slots = (blocks, 2, chips.links)
    landed = pl.pallas_call(
        functools.partial(flood, chips, rounds),
        out_shape=jax.ShapeDtypeStruct((blocks, TREES, rounds, STEP_ROWS, width), jnp.bfloat16),
        in_specs=[
            pl.BlockSpec(memory_space=pltpu.SMEM),
            pl.BlockSpec(memory_space=pltpu.SMEM),
            pl.BlockSpec(memory_space=pltpu.VMEM),
        ],
        out_specs=pl.BlockSpec(memory_space=pltpu.VMEM),
        scratch_shapes=[
            pltpu.VMEM(slots + (STEP_ROWS, width), jnp.bfloat16),
            pltpu.VMEM(slots + (STEP_ROWS, width), jnp.bfloat16),
            pltpu.SemaphoreType.DMA(slots),
            pltpu.SemaphoreType.DMA(slots),
        ],
        compiler_params=pltpu.CompilerParams(
            collective_id=0, has_side_effects=True, vmem_limit_bytes=32 * 1024 * 1024
        ),
        name="flood",
    )(my_parent, my_leaving, own)

    unit_rows = normalize(embeddings.astype(jnp.float32))
    parts = []
    for block in range(blocks):
        pieces = [
            lax.dynamic_slice(
                landed[block, tree], (my_depth[block, tree], 0, 0), (steps, STEP_ROWS, width)
            ).reshape(steps * STEP_ROWS, width)
            for tree in range(TREES)
        ]
        parts.append(jnp.concatenate(pieces)[:half])
    landmarks = jnp.concatenate(parts)
    cosine = jnp.einsum("rd,md->rm", unit_rows, landmarks, preferred_element_type=jnp.float32)
    mine = kernel_of(cosine, widths, weights).astype(jnp.bfloat16)
    other = lax.ppermute(mine, "bw", [(0, 1), (1, 0)])
    lower = jnp.where(core == 0, mine, other)
    upper = jnp.where(core == 0, other, mine)
    kernel = jnp.concatenate(
        [
            side[:, block * half : (block + 1) * half]
            for block in range(blocks)
            for side in (lower, upper)
        ],
        axis=1,
    )
    features = jnp.dot(kernel, whitening, preferred_element_type=jnp.float32)
    return features.astype(jnp.bfloat16)


def solution(mesh):
    chips = Chips(mesh.shape["row"], mesh.shape["lmk"])
    in_specs = (
        P(("row", "lmk"), None),
        P(("row", "lmk"), None),
        P(),
        P(),
        P("bw"),
        P("bw"),
        P(None, "bw"),
    )
    out_specs = P(("row", "lmk"), "bw")
    return jax.shard_map(
        functools.partial(per_device, chips),
        mesh=mesh,
        in_specs=in_specs,
        out_specs=out_specs,
        check_vma=False,
    )
```

time: 366 us -> 162 us (0.44)
  waiting for transfers between devices: 256 us -> 3.24 us
  Pallas kernels: 0 us -> 90.5 us
  local copies, waits for them, and re-layouts: 32.1 us -> 13.4 us
  blocking collectives: 20.4 us -> 2.65 us
  other arithmetic: 14.9 us -> 3.6 us
  matrix products: 24.2 us -> 30.2 us
    psum x1 -> x0, waiting for transfers between devices: 256 us -> none  [spread(): return lax.psum(block, axis)]
    pallas_call x0 -> x1, Pallas kernels: none -> 90.5 us  [per_device(): pl.pallas_call(functools.partial(flood, chips, rounds), out_shape=jax.Sha...]
    gather x2 -> x3, local copies, waits for them, and re-layouts: 27.4 us -> 4.45 us  [the longest x1 1.49 us: per_device(): my_parent = jnp.asarray(parent_link)[block_owner, me]]
    psum x1 -> x0, blocking collectives: 20.4 us -> none  [per_device(): kernel = lax.psum(partial_value, 'bw').astype(jnp.bfloat16)]
    dot_general x2, matrix products: 12.6 us -> 19 us  [the longest x1 10.5 us: per_device(): jnp.einsum('rd,md->rm', unit_rows, landmarks, preferred_element_type=jnp....]
    select_n x2, other arithmetic: 6.28 us -> 0.22 us  [the longest x1 0.21 us: per_device(): lower = jnp.where(core == 0, mine, other)]
    reduce_sum x2 -> x1, other arithmetic: 5.54 us -> 0.23 us  [normalize(): jnp.sum(widened * widened, axis=-1, keepdims=True) + 1e-06]
where the time goes in v1:
time: 162 us; the launch traced here: 161 us
  Pallas kernels  90.5 us (56%)
  matrix products  30.2 us (19%)
  between operations  17.6 us (11%)
  local copies, waits for them, and re-layouts  13.4 us (8%)
  other arithmetic  3.6 us (2%)
  waiting for transfers between devices  3.24 us (2%)
  blocking collectives  2.65 us (2%)
    pallas_call x1, Pallas kernels, per_device(): pl.pallas_call(functools.partial(flood, chips, rounds), out_shape=jax.Sha...  90.5 us
    dot_general x1, matrix products, per_device(): features = jnp.dot(kernel, whitening, preferred_element_type=jnp.float32)  11.2 us
    dot_general x1, matrix products, per_device(): jnp.einsum('rd,md->rm', unit_rows, landmarks, preferred_element_type=jnp....  10.5 us
    dot_general x1, matrix products, per_device(): jnp.dot(places, candidates, preferred_element_type=jnp.float32)  8.48 us
    ppermute x1, waiting for transfers between devices, per_device(): other = lax.ppermute(mine, 'bw', [(0, 1), (1, 0)])  3.24 us
  transfers between devices with their start and end apart: 1, of which 1 were waited for; matrix products, arithmetic and copies ran while one was open for 0% of the time, Pallas kernels for 0%

profile of v1, /device:TPU:0, one launch (start us, length us, event | category | flops | bytes accessed | tf_op | source)
XLA Modules:
  0.0 161.4 jit_solution(1860003148917601011)
XLA Ops:
  0.0 1.2 slice.113
  1.2 0.7 fusion.31
  1.9 1.5 gather_fusion.2
  3.4 0.7 fusion.39
  11.1 0.8 fusion.38
  11.9 8.5 %multiply_reduce_fusion = (f32[1024]{0:T(1024)S(1)}, f32[1024,1024]{1,0:T(8,128)}) fusion(bf16[2048,1024]{1,0:T(8,128)(2,1)} %param.11, s32[1024]{0:T(1024)S(1)} %bitcast.41), kind=kOutput, calls=%fused_computation.18 | convolution fusion | flops 4299160576 | bytes 8396800 | tf_op jit(solution)/shard_map/dot_general | solution.py:275
  20.4 1.5 gather_fusion
  21.9 1.5 gather_fusion.1
  23.4 2.5 %multiply_convert_fusion = bf16[1024,1024]{1,0:T(8,128)(2,1)S(1)} fusion(f32[1024,1024]{1,0:T(8,128)} %get-tuple-element.44, f32[1024]{0:T(1024)S(1)} %add_rsqrt_fusion), kind=kLoop, calls=%fused_computation.17 | loop fusion | flops 2097152 | bytes 6295552 | tf_op jit(solution)/shard_map/convert_element_type | solution.py:246
  25.9 0.2 pad.5
  26.1 90.5 %flood.1 = bf16[2,3,28,16,1024]{4,3,2,1,0:T(8,128)(2,1)S(1)} custom-call(s32[2,3]{1,0:T(2,128)S(1)} %gather_fusion, s32[2,4]{1,0:T(2,128)S(1)} %gather_fusion.1, bf16[3,22,16,1024]{3,2,1,0:T(8,128)(2,1)S(1)} %bitcast.34), custom_call_target="tpu_custom_call" | custom-call | tf_op jit(solution)/shard_map/flood/pallas_call | solution.py:284
  116.6 0.0 copy-start.4
  116.6 0.0 copy-start.2
  116.6 0.0 copy-start.3
  116.6 2.1 %fusion.35 = (bf16[1,1,28,16,1024]{4,3,2,1,0:T(8,128)(2,1)}, bf16[1,1,28,16,1024]{4,3,2,1,0:T(8,128)(2,1)S(1)}, bf16[1,1,28,16,1024]{4,3,2,1,0:T(8,128)(2,1)S(1)...) fusion(bf16[2,3,28,16,1024]{4,3,2,1,0:T(8,128)(2,1)S(1)} %flood.1), kind=kLoop, calls=%fused_computation.54 | loop fusion | bytes 11010048 | tf_op jit(solution)/shard_map/slice | solution.py:310
  119.3 0.6 dynamic-slice.7
  120.5 0.2 dynamic-update-slice
  120.8 0.2 dynamic-update-slice.1
  121.5 2.7 %all-reduce.4 = (f32[8]{0:T(128)S(1)}, f32[8]{0:T(128)S(1)}) all-reduce(f32[8]{0:T(128)S(1)} %dynamic-update-slice.1, f32[8]{0:T(128)S(1)} %dynamic-update-slice), channel_id=1, replica_groups=mesh['row'=4,'lmk'=4,'bw'=2] {'bw'}, use_global_device_ids=true, to_apply=%add.3 | all-reduce | flops 16 | bytes 128
  124.2 0.7 fusion.40
  129.9 0.2 fusion.23
  133.9 1.6 constant_dynamic-slice_fusion.4
  135.4 0.0 copy-done
  135.5 0.1 constant_dynamic-slice_fusion.2
  135.6 0.2 constant_dynamic-slice_fusion
  135.8 10.5 %add_convert_fusion = bf16[384,2048]{1,0:T(8,128)(2,1)S(1)} fusion(f32[]{:T(128)} %bitcast.31, f32[]{:T(128)} %bitcast.30, f32[]{:T(128)} %bitcast.29, f32[]{:T(128)} %bitcast.28, f32[]{:T(128)} %bitcast.27, f32[]{:T(128)} %bitcast.26, f32[]{:T(128)} %bitcast.25, f32[]{:T(128)} %bitcast.24, f32[]{:T(128)} %bitcast.23, f32[]{:T(128)} %bitcast.22, ...), kind=kOutput, calls=%fused_computation.28 | convolution fusion | flops 1660026880 | bytes 6686272 | tf_op jit(solution)/shard_map/rd,md->rm/dot_general | solution.py:316
  146.2 0.2 collective-permute-start
  146.5 3.2 %collective-permute-done = bf16[384,2048]{1,0:T(8,128)(2,1)S(1)} collective-permute-done((bf16[384,2048]{1,0:T(8,128)(2,1)S(1)}, bf16[384,2048]{1,0:T(8,128)(2,1)S(1)}, u32[]{:S(2)}, u32[]{:S(2)}) %collective-permute-start) | collective-permute-done | bytes 1572896 | tf_op jit(solution)/shard_map/ppermute | solution.py:318
  149.7 0.2 broadcast_select_fusion.1
  149.9 0.1 fusion.36
  150.1 0.1 fusion.37
  150.2 11.2 %fusion.19 = bf16[384,2048]{1,0:T(8,128)(2,1)} fusion(bf16[4096,2048]{1,0:T(8,128)(2,1)} %param.16, bf16[384,1024]{1,0:T(8,128)(2,1)S(1)} %get-tuple-element.18, bf16[384,1024]{1,0:T(8,128)(2,1)S(1)} %get-tuple-element.16, bf16[384,1024]{1,0:T(8,128)(2,1)S(1)} %get-tuple-element.17, bf16[384,1024]{1,0:T(8,128)(2,1)S(1)} %get-tuple-element.15), kind=kOutput, calls=%fused_computation.29 | convolution fusion | flops 6455820288 | bytes 21495808 | tf_op jit(solution)/shard_map/dot_general | solution.py:329
  (11 shorter events, 0.0 us)
Async XLA Ops:
  116.6 2.7 %copy-start.4 = (u32[32]{0:T(128)S(1)}, u32[32]{0:T(128)}, u32[]{:S(2)}) copy-start(u32[32]{0:T(128)} %constant.103) | copy-start | bytes 388
  116.6 3.9 %copy-start.2 = (f32[4]{0:T(128)S(1)}, f32[4]{0:T(128)}, u32[]{:S(2)}) copy-start(f32[4]{0:T(128)} %param.15) | copy-start | bytes 52
  116.6 4.2 %copy-start.3 = (f32[4]{0:T(128)S(1)}, f32[4]{0:T(128)}, u32[]{:S(2)}) copy-start(f32[4]{0:T(128)} %param.14) | copy-start | bytes 52
  116.6 13.2 %copy-start.1 = (bf16[384,1024]{1,0:T(8,128)(2,1)S(1)}, bf16[384,1024]{1,0:T(8,128)(2,1)}, u32[]{:S(2)}) copy-start(bf16[384,1024]{1,0:T(8,128)(2,1)} %param.10) | copy-start | bytes 2359300
  133.8 1.6 copy-start
  146.2 3.5 %collective-permute-start = (bf16[384,2048]{1,0:T(8,128)(2,1)S(1)}, bf16[384,2048]{1,0:T(8,128)(2,1)S(1)}, u32[]{:S(2)}, u32[]{:S(2)}) collective-permute-start(bf16[384,2048]{1,0:T(8,128)(2,1)S(1)} %add_convert_fusion), channel_id=1, source_target_pairs={{0,1},{1,0},{2,3},{3,2},{4,5},{5,4},{6,7},{7,6},{8,9},{9,8},{10,11... | collective-permute-start | bytes 4718600 | tf_op jit(solution)/shard_map/ppermute | solution.py:318

commit v2 on v1

--- a/solution.py
+++ b/solution.py
@@ -1,4 +1,5 @@
 import functools
+import math
 import random
 
 import jax
@@ -11,7 +12,7 @@
 
 MESH = pl.DeviceIdType.MESH
 TREES = 3
-STEP_ROWS = 16
+STEP_ROWS = 32
 
 
 class Chips:
@@ -152,10 +153,22 @@
     return parent_link, depth, leaving
 
 
-def flood(chips, rounds, parent_ref, leaving_ref, own_ref, land_ref, arrive, leave, send_sem, recv_sem):
-    row, lmk = lax.axis_index("row"), lax.axis_index("lmk")
-    steps = own_ref.shape[1]
-    blocks = land_ref.shape[0]
+def fused(
+    chips, rounds, deepest,
+    owner_ref, table_ref, picks_ref, params_ref, rows_ref, candidates_ref, whitening_ref,
+    features_ref,
+    own, land, arrive, leave, columns, places, product, unit, fresh, cosine, mine, other, factor, total, held, theirs,
+    send_sem, recv_sem, mine_sem, other_sem, params_sem, held_sem,
+):
+    row, lmk, core = lax.axis_index("row"), lax.axis_index("lmk"), lax.axis_index("bw")
+    me = row * chips.lmks + lmk
+    blocks = owner_ref.shape[0]
+    block_rows, width = candidates_ref.shape
+    half = block_rows // 2
+    row_count, feature_count = total.shape
+    span = TREES * STEP_ROWS
+    steps = -(-half // span)
+    partner = {"bw": 1 - core}
 
     def each_link(act):
         for link in range(chips.links):
@@ -169,48 +182,122 @@
         r, k = chips.neighbour(link, row, lmk)
         return {"row": r, "lmk": k}
 
-    def outgoing(block, slot, link):
+    def copy_to(link, block, slot, arriving):
         return pltpu.make_async_remote_copy(
             src_ref=leave.at[block, slot, link],
-            dst_ref=arrive.at[block, slot, chips.back[link]],
+            dst_ref=arrive.at[block, slot, arriving],
             send_sem=send_sem.at[block, slot, link],
-            recv_sem=recv_sem.at[block, slot, chips.back[link]],
+            recv_sem=recv_sem.at[block, slot, arriving],
             device_id=target(link),
             device_id_type=MESH,
         )
 
+    def outgoing(block, slot, link):
+        return copy_to(link, block, slot, chips.back[link])
+
     def incoming(block, slot, link):
+        return copy_to(link, block, slot, link)
+
+    def share(step):
         return pltpu.make_async_remote_copy(
-            src_ref=leave.at[block, slot, link],
-            dst_ref=arrive.at[block, slot, link],
-            send_sem=send_sem.at[block, slot, link],
-            recv_sem=recv_sem.at[block, slot, link],
-            device_id=target(link),
+            src_ref=mine.at[step],
+            dst_ref=other.at[step + 1],
+            send_sem=mine_sem.at[step],
+            recv_sem=other_sem.at[step],
+            device_id=partner,
             device_id_type=MESH,
         )
 
+    params_copy = pltpu.make_async_remote_copy(
+        src_ref=params_ref,
+        dst_ref=theirs,
+        send_sem=params_sem.at[0],
+        recv_sem=params_sem.at[1],
+        device_id=partner,
+        device_id_type=MESH,
+    )
+    whole_rows = whitening_ref.shape[0]
+    whitening_copy = pltpu.make_async_copy(whitening_ref, held.at[pl.ds(0, whole_rows)], held_sem)
+
     barrier = pltpu.get_barrier_semaphore()
 
     def greet(link):
         pl.semaphore_signal(barrier, inc=1, device_id=target(link), device_id_type=MESH)
 
     each_link(greet)
-    pl.semaphore_wait(barrier, chips.degree(lmk))
-
-    def one_round(step, first, last):
+    pl.semaphore_signal(barrier, inc=1, device_id=partner, device_id_type=MESH)
+    whitening_copy.start()
+
+    first_word, second_word = [], []
+    for block in range(blocks):
+        at = 2 * (owner_ref[block] * chips.count + me)
+        first_word.append(table_ref[at])
+        second_word.append(table_ref[at + 1])
+
+    def parent(block, tree):
+        return (first_word[block] >> (3 * tree)) & 7
+
+    def depth(block, tree):
+        return (first_word[block] >> (9 + 4 * tree)) & 15
+
+    def leaving(block, link):
+        return (second_word[block] >> (2 * link)) & 3
+
+    picked = lax.select(owner_ref[1] == me, picks_ref[1, core], picks_ref[0, core])
+    for group in range(half // 128):
+        columns[group * 128 : (group + 1) * 128] = jnp.transpose(
+            jnp.broadcast_to(picked[group : group + 1], (128, 128))
+        )
+    columns[half:] = jnp.zeros_like(columns[half:])
+
+    def normalize(widened):
+        scale = lax.rsqrt(jnp.sum(widened * widened, axis=-1, keepdims=True) + 1e-06)
+        return (widened * scale).astype(jnp.bfloat16)
+
+    def gather(group):
+        size = places.shape[0]
+        lanes = lax.broadcasted_iota(jnp.int32, (size, 128), 1)
+        wanted = columns[group * size : (group + 1) * size]
+        for tile in range(block_rows // 128):
+            places[:, tile * 128 : (tile + 1) * 128] = jnp.where(
+                wanted == lanes + tile * 128, 1.0, 0.0
+            ).astype(jnp.bfloat16)
+
+        def tile_of(tile, carry):
+            cols = pl.ds(pl.multiple_of(tile * 256, 256), 256)
+            product[:, cols] = jnp.dot(
+                places[...], candidates_ref[:, cols], preferred_element_type=jnp.float32
+            )
+            return carry
+
+        lax.fori_loop(0, width // 256, tile_of, 0)
+
+        def piece(index, carry):
+            rows = pl.ds(pl.multiple_of(index * STEP_ROWS, STEP_ROWS), STEP_ROWS)
+            own[group * (size // STEP_ROWS) + index] = normalize(product[rows])
+            return carry
+
+        lax.fori_loop(0, size // STEP_ROWS, piece, 0)
+
+    groups = own.shape[0] * STEP_ROWS // places.shape[0]
+    gather(0)
+    pl.semaphore_wait(barrier, chips.degree(lmk) + 1)
+    params_copy.start()
+
+    def pass_on(step, first, last):
         slot, before = step % 2, (step + 1) % 2
         for block in range(blocks):
             if not first:
                 each_link(lambda link: incoming(block, before, link).wait_recv())
-            held = []
+            values = []
             for tree in range(TREES):
-                origin = parent_ref[block, tree]
-                value = own_ref[tree, jnp.minimum(step, steps - 1)]
+                origin = parent(block, tree)
+                value = own[jnp.minimum(step, steps - 1) * TREES + tree]
                 if not first:
                     for link in range(chips.links):
-                        value = lax.select(origin == link, arrive[block, before, link], value)
-                land_ref[block, tree, step] = value
-                held.append(value)
+                        value = lax.select(origin == link + 1, arrive[block, before, link], value)
+                land[block, tree, step] = value
+                values.append(value)
             if last:
                 continue
 
@@ -221,113 +308,186 @@
                     def _():
                         outgoing(block, slot, link).wait_send()
 
-                tree = leaving_ref[block, link]
-                value = lax.select(tree == 1, held[1], held[0])
-                leave[block, slot, link] = lax.select(tree == 2, held[2], value)
+                tree = leaving(block, link)
+                value = lax.select(tree == 1, values[1], values[0])
+                leave[block, slot, link] = lax.select(tree == 2, values[2], value)
                 outgoing(block, slot, link).start()
 
             each_link(send)
 
-    one_round(0, True, False)
+    def kernel_step(step):
+        for block in range(blocks):
+            for tree in range(TREES):
+                fresh[pl.ds(block * span + tree * STEP_ROWS, STEP_ROWS)] = land[
+                    block, tree, step + depth(block, tree)
+                ]
+        cosine[...] = lax.dot_general(
+            unit[...], fresh[...], (((1,), (1,)), ((), ())), preferred_element_type=jnp.float32
+        )
+        spreads = params_ref.shape[0] // 2
+        pairs = [
+            [jnp.concatenate([ref[at : at + 1]] * (cosine.shape[1] // 128), axis=1) for at in (s, s + spreads)]
+            for ref in (params_ref, theirs)
+            for s in range(spreads)
+        ]
+
+        def strip(index, carry):
+            rows = pl.ds(pl.multiple_of(index * 32, 32), 32)
+            value = cosine[rows]
+            running = jnp.zeros_like(value)
+            for width_of, weight_of in pairs:
+                running = running + weight_of * jnp.exp2(width_of * value)
+            mine[step, rows] = running.astype(jnp.bfloat16)
+            return carry
+
+        lax.fori_loop(0, row_count // 32, strip, 0)
+        share(step).start()
+
+    def factor_rows(at, step, side):
+        for block in range(blocks):
+            for tree in range(TREES):
+                start = block * block_rows + side * half + step * span + tree * STEP_ROWS
+                value = held[pl.ds(pl.multiple_of(start, STEP_ROWS), STEP_ROWS)]
+                if (steps - 1) * span + tree * STEP_ROWS >= half:
+                    value = lax.select(step < steps - 1, value, jnp.zeros_like(value))
+                to = at + block * span + tree * STEP_ROWS
+                factor[to : to + STEP_ROWS] = value
+
+    def feature_step(left):
+        def tile_of(tile, carry):
+            cols = pl.ds(pl.multiple_of(tile * 512, 512), 512)
+            total[:, cols] += jnp.dot(
+                left, factor[: left.shape[1], cols], preferred_element_type=jnp.float32
+            )
+            return carry
+
+        lax.fori_loop(0, feature_count // 512, tile_of, 0)
+
+    pass_on(0, True, False)
+    for group in range(1, groups - 1):
+        gather(group)
+
+    def unit_piece(index, carry):
+        rows = pl.ds(pl.multiple_of(index * 32, 32), 32)
+        unit[rows] = normalize(rows_ref[rows].astype(jnp.float32))
+        return carry
+
+    pass_on(1, False, False)
+    gather(groups - 1)
+    pass_on(2, False, False)
+    lax.fori_loop(0, row_count // 32, unit_piece, 0)
+    fresh[...] = jnp.zeros_like(fresh)
+    factor[...] = jnp.zeros_like(factor)
+    total[...] = jnp.zeros_like(total)
+    other[0] = jnp.zeros_like(other[0])
+    params_copy.wait()
+
+    def early(step, carry):
+        pass_on(step, False, False)
+        return carry
+
+    lax.fori_loop(3, deepest, early, 0)
+    whitening_copy.wait()
+    padded = mine.shape[2]
+
+    def work(step):
+        kernel_step(step)
+
+        @pl.when(step >= 1)
+        def _():
+            share(step - 1).wait_recv()
+
+        factor_rows(0, step, core)
+        factor_rows(padded, jnp.maximum(step - 1, 0), 1 - core)
+        feature_step(jnp.concatenate([mine[step], other[step]], axis=1))
 
     def middle(step, carry):
-        one_round(step, False, False)
+        pass_on(step, False, False)
+        work(step - deepest)
         return carry
 
-    lax.fori_loop(1, rounds - 1, middle, 0)
-    one_round(rounds - 1, False, True)
+    lax.fori_loop(deepest, rounds - 1, middle, 0)
+    pass_on(rounds - 1, False, True)
+    work(steps - 1)
+    share(steps - 1).wait_recv()
+    factor_rows(0, steps - 1, 1 - core)
+    feature_step(other[steps])
+    features_ref[...] = total[...].astype(jnp.bfloat16)
+
     for block in range(blocks):
         for slot in range(2):
             each_link(lambda link: outgoing(block, slot, link).wait_send())
 
-
-def normalize(widened):
-    scale = lax.rsqrt(jnp.sum(widened * widened, axis=-1, keepdims=True) + 1e-06)
-    return (widened * scale).astype(jnp.bfloat16)
-
-
-def kernel_of(cosine, widths, weights):
-    running = jnp.zeros(cosine.shape, jnp.float32)
-    for which in range(widths.shape[0]):
-        running = running + weights[which] * jnp.exp(2.0 * widths[which] * cosine)
-    return running
+    def sent(step, carry):
+        share(step).wait_send()
+        return carry
+
+    lax.fori_loop(0, steps, sent, 0)
 
 
 def per_device(
     chips, embeddings, candidates, block_owner, landmark_picks, inverse_width, mixture, whitening
 ):
-    me = lax.axis_index("row") * chips.lmks + lax.axis_index("lmk")
-    core = lax.axis_index("bw")
     blocks, block_rows = landmark_picks.shape
-    width = embeddings.shape[1]
+    row_count, width = embeddings.shape
+    feature_count = whitening.shape[1]
     half = block_rows // 2
-    steps = -(-half // (TREES * STEP_ROWS))
+    span = TREES * STEP_ROWS
+    steps = -(-half // span)
     parent_link, depth, leaving = routes(chips.rows, chips.lmks)
     deepest = int(depth.max())
     rounds = steps + deepest
-
-    widths = lax.all_gather(inverse_width, "bw", tiled=True)
-    weights = lax.all_gather(mixture, "bw", tiled=True)
-
-    picks = jnp.where(block_owner[1] == me, landmark_picks[1], landmark_picks[0])
-    picks = lax.dynamic_slice(picks, (core * half,), (half,))
-    places = (picks[:, None] == jnp.arange(block_rows, dtype=jnp.int32)[None, :]).astype(jnp.bfloat16)
-    chosen = normalize(jnp.dot(places, candidates, preferred_element_type=jnp.float32))
-    own = jnp.pad(chosen, ((0, TREES * steps * STEP_ROWS - half), (0, 0)))
-    own = own.reshape(TREES, steps, STEP_ROWS, width)
-
-    my_parent = jnp.asarray(parent_link)[block_owner, me]
-    my_depth = jnp.asarray(depth)[block_owner, me]
-    my_leaving = jnp.asarray(leaving)[block_owner, me]
+    padded = -(-blocks * span // 128) * 128
+    group_rows = 4 * span
+    own_rows = -(-half // group_rows) * group_rows
+
+    first = sum((parent_link[..., t] + 1) << (3 * t) for t in range(TREES))
+    first = first + sum(depth[..., t] << (9 + 4 * t) for t in range(TREES))
+    second = sum(leaving[..., link] << (2 * link) for link in range(chips.links))
+    table = np.stack([first, second], axis=-1).reshape(-1).astype(np.int32)
+
+    params = jnp.concatenate([inverse_width * (2.0 * math.log2(math.e)), mixture])
+    params = jnp.broadcast_to(params[:, None], (params.shape[0], 128))
+    picks = landmark_picks.reshape(blocks, 2, half // 128, 128)
 
     slots = (blocks, 2, chips.links)
-    landed = pl.pallas_call(
-        functools.partial(flood, chips, rounds),
-        out_shape=jax.ShapeDtypeStruct((blocks, TREES, rounds, STEP_ROWS, width), jnp.bfloat16),
-        in_specs=[
-            pl.BlockSpec(memory_space=pltpu.SMEM),
-            pl.BlockSpec(memory_space=pltpu.SMEM),
-            pl.BlockSpec(memory_space=pltpu.VMEM),
-        ],
-        out_specs=pl.BlockSpec(memory_space=pltpu.VMEM),
+    bf16, f32 = jnp.bfloat16, jnp.float32
+    in_vmem = pl.BlockSpec(memory_space=pltpu.VMEM)
+    in_smem = pl.BlockSpec(memory_space=pltpu.SMEM)
+    return pl.pallas_call(
+        functools.partial(fused, chips, rounds, deepest),
+        out_shape=jax.ShapeDtypeStruct((row_count, feature_count), bf16),
+        in_specs=[in_smem, in_smem] + [in_vmem] * 4 + [pl.BlockSpec(memory_space=pl.ANY)],
+        out_specs=in_vmem,
         scratch_shapes=[
-            pltpu.VMEM(slots + (STEP_ROWS, width), jnp.bfloat16),
-            pltpu.VMEM(slots + (STEP_ROWS, width), jnp.bfloat16),
+            pltpu.VMEM((own_rows // STEP_ROWS, STEP_ROWS, width), bf16),
+            pltpu.VMEM((blocks, TREES, rounds, STEP_ROWS, width), bf16),
+            pltpu.VMEM(slots + (STEP_ROWS, width), bf16),
+            pltpu.VMEM(slots + (STEP_ROWS, width), bf16),
+            pltpu.VMEM((own_rows, 128), jnp.int32),
+            pltpu.VMEM((group_rows, block_rows), bf16),
+            pltpu.VMEM((group_rows, width), f32),
+            pltpu.VMEM((row_count, width), bf16),
+            pltpu.VMEM((padded, width), bf16),
+            pltpu.VMEM((row_count, padded), f32),
+            pltpu.VMEM((steps, row_count, padded), bf16),
+            pltpu.VMEM((steps + 1, row_count, padded), bf16),
+            pltpu.VMEM((2 * padded, feature_count), bf16),
+            pltpu.VMEM((row_count, feature_count), f32),
+            pltpu.VMEM((whitening.shape[0] + STEP_ROWS, feature_count), bf16),
+            pltpu.VMEM(params.shape, f32),
             pltpu.SemaphoreType.DMA(slots),
             pltpu.SemaphoreType.DMA(slots),
+            pltpu.SemaphoreType.DMA((steps,)),
+            pltpu.SemaphoreType.DMA((steps,)),
+            pltpu.SemaphoreType.DMA((2,)),
+            pltpu.SemaphoreType.DMA,
         ],
         compiler_params=pltpu.CompilerParams(
-            collective_id=0, has_side_effects=True, vmem_limit_bytes=32 * 1024 * 1024
+            collective_id=0, has_side_effects=True, vmem_limit_bytes=60 * 1024 * 1024
         ),
-        name="flood",
-    )(my_parent, my_leaving, own)
-
-    unit_rows = normalize(embeddings.astype(jnp.float32))
-    parts = []
-    for block in range(blocks):
-        pieces = [
-            lax.dynamic_slice(
-                landed[block, tree], (my_depth[block, tree], 0, 0), (steps, STEP_ROWS, width)
-            ).reshape(steps * STEP_ROWS, width)
-            for tree in range(TREES)
-        ]
-        parts.append(jnp.concatenate(pieces)[:half])
-    landmarks = jnp.concatenate(parts)
-    cosine = jnp.einsum("rd,md->rm", unit_rows, landmarks, preferred_element_type=jnp.float32)
-    mine = kernel_of(cosine, widths, weights).astype(jnp.bfloat16)
-    other = lax.ppermute(mine, "bw", [(0, 1), (1, 0)])
-    lower = jnp.where(core == 0, mine, other)
-    upper = jnp.where(core == 0, other, mine)
-    kernel = jnp.concatenate(
-        [
-            side[:, block * half : (block + 1) * half]
-            for block in range(blocks)
-            for side in (lower, upper)
-        ],
-        axis=1,
-    )
-    features = jnp.dot(kernel, whitening, preferred_element_type=jnp.float32)
-    return features.astype(jnp.bfloat16)
+        name="fused",
+    )(block_owner, jnp.asarray(table), picks, params, embeddings, candidates, whitening)
 
 
 def solution(mesh):

time: 162 us -> 86.3 us (0.53)
  matrix products: 30.2 us -> 0 us
  between operations: 17.6 us -> 0.01 us
  Pallas kernels: 90.5 us -> 80 us
  local copies, waits for them, and re-layouts: 13.4 us -> 4.71 us
  waiting for transfers between devices: 3.24 us -> 0 us
  blocking collectives: 2.65 us -> 0 us
  other arithmetic: 3.6 us -> 1.39 us
    dot_general x3 -> x0, matrix products: 30.2 us -> none  [the longest x1 11.2 us: per_device(): features = jnp.dot(kernel, whitening, preferred_element_type=jnp.float32)]
    pallas_call x1, Pallas kernels: 90.5 us -> 80 us  [per_device(): pl.pallas_call(functools.partial(fused, chips, rounds, deepest), out_shap...]
    slice x7 -> x0, local copies, waits for them, and re-layouts: 5.73 us -> none  [the longest x1 2.06 us: per_device(): landed[block, tree]]
    gather x3 -> x0, local copies, waits for them, and re-layouts: 4.45 us -> none  [the longest x1 1.49 us: per_device(): my_parent = jnp.asarray(parent_link)[block_owner, me]]
    ppermute x1 -> x0, waiting for transfers between devices: 3.24 us -> none  [per_device(): other = lax.ppermute(mine, 'bw', [(0, 1), (1, 0)])]
    unnamed x15 -> x2, local copies, waits for them, and re-layouts: 1.14 us -> 4.05 us
    unnamed x1 -> x0, blocking collectives: 2.65 us -> none
    convert_element_type x1 -> x0, other arithmetic: 2.48 us -> none  [normalize(): return (widened * scale).astype(jnp.bfloat16)]
  transfers between devices with their start and end apart: 1 -> 0, of which waited for: 1 -> 0; matrix products, arithmetic and copies ran while one was open for 0% -> 0% of each run, Pallas kernels for 0% -> 0%
where the time goes in v2:
time: 86.3 us; the launch traced here: 86.1 us
  Pallas kernels  80 us (93%)
  local copies, waits for them, and re-layouts  4.71 us (5%)
  other arithmetic  1.39 us (2%)
    pallas_call x1, Pallas kernels, per_device(): pl.pallas_call(functools.partial(fused, chips, rounds, deepest), out_shap...  80 us
    unnamed x2, local copies, waits for them, and re-layouts  4.05 us

profile of v2, /device:TPU:0, one launch (start us, length us, event | category | flops | bytes accessed | tf_op | source)
XLA Modules:
  0.0 86.1 jit_solution(17290817963884996103)
XLA Ops:
  0.0 0.7 broadcast_multiply_fusion
  0.7 0.7 pad_maximum_fusion
  1.4 0.7 broadcast_in_dim.2.params_ref
  2.0 1.3 %copy.11 = s32[1,2,16,128]{3,2,1,0:T(8,128)} copy(s32[1,2,16,128]{3,1,2,0:T(2,128)} %bitcast.6) | data formatting | bytes 32768
  3.4 80.0 %fused.1 = bf16[384,2048]{1,0:T(8,128)(2,1)} custom-call(s32[2]{0:T(128)} %owner_ref.1, s32[512]{0:T(512)} %constant.4.clone.table_ref, s32[2,2,8,128]{3,2,1,0:T(8,128)} %bitcast.5, f32[8,128]{1,0:T(8,128)} %broadcast_in_dim.2.params_ref, bf16[384,1024]{1,0:T(8,128)(2,1)} %rows_ref.1, bf16[2048,1024]{1,0:T(8,128)(2,1)} %candidates_ref.1, ...), custom_call_target="tpu_custom_call" | custom-call | tf_op jit(solution)/shard_map/fused/pallas_call | solution.py:457
  83.3 2.7 %copy.13 = bf16[384,2048]{1,0:T(8,128)(2,1)} copy(bf16[384,2048]{1,0:T(8,128)(2,1)} %fused.1) | data formatting | bytes 3145728

commit v3 on v2

--- a/solution.py
+++ b/solution.py
@@ -155,9 +155,9 @@
 
 def fused(
     chips, rounds, deepest,
-    owner_ref, table_ref, picks_ref, params_ref, rows_ref, candidates_ref, whitening_ref,
+    owner_ref, table_ref, widths_ref, weights_ref, picks_ref, rows_ref, candidates_ref, whitening_ref,
     features_ref,
-    own, land, arrive, leave, columns, places, product, unit, fresh, cosine, mine, other, factor, total, held, theirs,
+    own, land, arrive, leave, columns, places, product, unit, fresh, cosine, mine, other, factor, total, held, params_ref, theirs,
     send_sem, recv_sem, mine_sem, other_sem, params_sem, held_sem,
 ):
     row, lmk, core = lax.axis_index("row"), lax.axis_index("lmk"), lax.axis_index("bw")
@@ -243,11 +243,10 @@
     def leaving(block, link):
         return (second_word[block] >> (2 * link)) & 3
 
-    picked = lax.select(owner_ref[1] == me, picks_ref[1, core], picks_ref[0, core])
     for group in range(half // 128):
-        columns[group * 128 : (group + 1) * 128] = jnp.transpose(
-            jnp.broadcast_to(picked[group : group + 1], (128, 128))
-        )
+        lanes_of = pl.ds(pl.multiple_of(core * half + group * 128, 128), 128)
+        picked = lax.select(owner_ref[1] == me, picks_ref[1:2, lanes_of], picks_ref[0:1, lanes_of])
+        columns[group * 128 : (group + 1) * 128] = jnp.transpose(jnp.broadcast_to(picked, (128, 128)))
     columns[half:] = jnp.zeros_like(columns[half:])
 
     def normalize(widened):
@@ -279,41 +278,45 @@
 
         lax.fori_loop(0, size // STEP_ROWS, piece, 0)
 
+    spreads = widths_ref.shape[0]
+    for s in range(spreads):
+        params_ref[s : s + 1] = jnp.full((1, 128), widths_ref[s] * (2.0 * math.log2(math.e)), jnp.float32)
+        params_ref[spreads + s : spreads + s + 1] = jnp.full((1, 128), weights_ref[s], jnp.float32)
+
     groups = own.shape[0] * STEP_ROWS // places.shape[0]
     gather(0)
     pl.semaphore_wait(barrier, chips.degree(lmk) + 1)
     params_copy.start()
 
-    def pass_on(step, first, last):
+    def pass_on(block, step, first=False, last=False):
         slot, before = step % 2, (step + 1) % 2
-        for block in range(blocks):
+        if not first:
+            each_link(lambda link: incoming(block, before, link).wait_recv())
+        values = []
+        for tree in range(TREES):
+            origin = parent(block, tree)
+            value = own[jnp.minimum(step, steps - 1) * TREES + tree]
             if not first:
-                each_link(lambda link: incoming(block, before, link).wait_recv())
-            values = []
-            for tree in range(TREES):
-                origin = parent(block, tree)
-                value = own[jnp.minimum(step, steps - 1) * TREES + tree]
-                if not first:
-                    for link in range(chips.links):
-                        value = lax.select(origin == link + 1, arrive[block, before, link], value)
-                land[block, tree, step] = value
-                values.append(value)
-            if last:
-                continue
-
-            def send(link):
-                if not first:
-
-                    @pl.when(step >= 2)
-                    def _():
-                        outgoing(block, slot, link).wait_send()
-
-                tree = leaving(block, link)
-                value = lax.select(tree == 1, values[1], values[0])
-                leave[block, slot, link] = lax.select(tree == 2, values[2], value)
-                outgoing(block, slot, link).start()
-
-            each_link(send)
+                for link in range(chips.links):
+                    value = lax.select(origin == link + 1, arrive[block, before, link], value)
+            land[block, tree, step] = value
+            values.append(value)
+        if last:
+            return
+
+        def send(link):
+            if not first:
+
+                @pl.when(step >= 2)
+                def _():
+                    outgoing(block, slot, link).wait_send()
+
+            tree = leaving(block, link)
+            value = lax.select(tree == 1, values[1], values[0])
+            leave[block, slot, link] = lax.select(tree == 2, values[2], value)
+            outgoing(block, slot, link).start()
+
+        each_link(send)
 
     def kernel_step(step):
         for block in range(blocks):
@@ -324,7 +327,6 @@
         cosine[...] = lax.dot_general(
             unit[...], fresh[...], (((1,), (1,)), ((), ())), preferred_element_type=jnp.float32
         )
-        spreads = params_ref.shape[0] // 2
         pairs = [
             [jnp.concatenate([ref[at : at + 1]] * (cosine.shape[1] // 128), axis=1) for at in (s, s + spreads)]
             for ref in (params_ref, theirs)
@@ -363,36 +365,37 @@
 
         lax.fori_loop(0, feature_count // 512, tile_of, 0)
 
-    pass_on(0, True, False)
-    for group in range(1, groups - 1):
-        gather(group)
-
     def unit_piece(index, carry):
         rows = pl.ds(pl.multiple_of(index * 32, 32), 32)
         unit[rows] = normalize(rows_ref[rows].astype(jnp.float32))
         return carry
 
-    pass_on(1, False, False)
+    pass_on(0, 0, first=True)
+    pass_on(1, 0, first=True)
+    for group in range(1, groups - 1):
+        gather(group)
+    pass_on(0, 1)
     gather(groups - 1)
-    pass_on(2, False, False)
+    pass_on(1, 1)
+    pass_on(0, 2)
     lax.fori_loop(0, row_count // 32, unit_piece, 0)
     fresh[...] = jnp.zeros_like(fresh)
+    pass_on(1, 2)
     factor[...] = jnp.zeros_like(factor)
     total[...] = jnp.zeros_like(total)
     other[0] = jnp.zeros_like(other[0])
     params_copy.wait()
 
     def early(step, carry):
-        pass_on(step, False, False)
+        pass_on(0, step)
+        pass_on(1, step)
         return carry
 
     lax.fori_loop(3, deepest, early, 0)
     whitening_copy.wait()
     padded = mine.shape[2]
 
-    def work(step):
-        kernel_step(step)
-
+    def features_of(step):
         @pl.when(step >= 1)
         def _():
             share(step - 1).wait_recv()
@@ -401,14 +404,23 @@
         factor_rows(padded, jnp.maximum(step - 1, 0), 1 - core)
         feature_step(jnp.concatenate([mine[step], other[step]], axis=1))
 
+    pass_on(0, deepest)
+    pass_on(1, deepest)
+    kernel_step(0)
+
     def middle(step, carry):
-        pass_on(step, False, False)
-        work(step - deepest)
+        pass_on(0, step)
+        features_of(step - deepest - 1)
+        pass_on(1, step)
+        kernel_step(step - deepest)
         return carry
 
-    lax.fori_loop(deepest, rounds - 1, middle, 0)
-    pass_on(rounds - 1, False, True)
-    work(steps - 1)
+    lax.fori_loop(deepest + 1, rounds - 1, middle, 0)
+    pass_on(0, rounds - 1, last=True)
+    features_of(steps - 2)
+    pass_on(1, rounds - 1, last=True)
+    kernel_step(steps - 1)
+    features_of(steps - 1)
     share(steps - 1).wait_recv()
     factor_rows(0, steps - 1, 1 - core)
     feature_step(other[steps])
@@ -446,10 +458,6 @@
     second = sum(leaving[..., link] << (2 * link) for link in range(chips.links))
     table = np.stack([first, second], axis=-1).reshape(-1).astype(np.int32)
 
-    params = jnp.concatenate([inverse_width * (2.0 * math.log2(math.e)), mixture])
-    params = jnp.broadcast_to(params[:, None], (params.shape[0], 128))
-    picks = landmark_picks.reshape(blocks, 2, half // 128, 128)
-
     slots = (blocks, 2, chips.links)
     bf16, f32 = jnp.bfloat16, jnp.float32
     in_vmem = pl.BlockSpec(memory_space=pltpu.VMEM)
@@ -457,7 +465,7 @@
     return pl.pallas_call(
         functools.partial(fused, chips, rounds, deepest),
         out_shape=jax.ShapeDtypeStruct((row_count, feature_count), bf16),
-        in_specs=[in_smem, in_smem] + [in_vmem] * 4 + [pl.BlockSpec(memory_space=pl.ANY)],
+        in_specs=[in_smem] * 4 + [in_vmem] * 3 + [pl.BlockSpec(memory_space=pl.ANY)],
         out_specs=in_vmem,
         scratch_shapes=[
             pltpu.VMEM((own_rows // STEP_ROWS, STEP_ROWS, width), bf16),
@@ -475,7 +483,8 @@
             pltpu.VMEM((2 * padded, feature_count), bf16),
             pltpu.VMEM((row_count, feature_count), f32),
             pltpu.VMEM((whitening.shape[0] + STEP_ROWS, feature_count), bf16),
-            pltpu.VMEM(params.shape, f32),
+            pltpu.VMEM((2 * inverse_width.shape[0], 128), f32),
+            pltpu.VMEM((2 * inverse_width.shape[0], 128), f32),
             pltpu.SemaphoreType.DMA(slots),
             pltpu.SemaphoreType.DMA(slots),
             pltpu.SemaphoreType.DMA((steps,)),
@@ -487,7 +496,7 @@
             collective_id=0, has_side_effects=True, vmem_limit_bytes=60 * 1024 * 1024
         ),
         name="fused",
-    )(block_owner, jnp.asarray(table), picks, params, embeddings, candidates, whitening)
+    )(block_owner, jnp.asarray(table), inverse_width, mixture, landmark_picks, embeddings, candidates, whitening)
 
 
 def solution(mesh):

time: 86.3 us -> 83.5 us (0.968)
  local copies, waits for them, and re-layouts: 4.71 us -> 2.73 us
  other arithmetic: 1.39 us -> 0 us
    unnamed x2 -> x1, local copies, waits for them, and re-layouts: 4.05 us -> 2.73 us
where the time goes in v3:
time: 83.5 us; the launch traced here: 83.3 us
  Pallas kernels  80.6 us (97%)
  local copies, waits for them, and re-layouts  2.73 us (3%)
    pallas_call x1, Pallas kernels, per_device(): pl.pallas_call(functools.partial(fused, chips, rounds, deepest), out_shap...  80.6 us
    unnamed x1, local copies, waits for them, and re-layouts  2.73 us

profile of v3, /device:TPU:0, one launch (start us, length us, event | category | flops | bytes accessed | tf_op | source)
XLA Modules:
  0.0 83.3 jit_solution(4213473861167998543)
XLA Ops:
  0.0 80.6 %fused.1 = bf16[384,2048]{1,0:T(8,128)(2,1)} custom-call(s32[2]{0:T(128)} %owner_ref.1, s32[512]{0:T(512)} %constant.2.clone.table_ref, f32[4]{0:T(128)} %widths_ref.1, f32[4]{0:T(128)} %weights_ref.1, s32[2,2048]{1,0:T(2,128)} %picks_ref.1, bf16[384,1024]{1,0:T(8,128)(2,1)} %rows_ref.1, bf16[2048,1024]{1,0:T(8,128)(2,1)} %candidates_ref.1, ...), custom_call_target="tpu_custom_call" | custom-call | tf_op jit(solution)/shard_map/fused/pallas_call | solution.py:465
  80.6 2.7 %copy.10 = bf16[384,2048]{1,0:T(8,128)(2,1)} copy(bf16[384,2048]{1,0:T(8,128)(2,1)} %fused.1) | data formatting | bytes 3145728

commit v4 on v3

--- a/solution.py
+++ b/solution.py
@@ -12,7 +12,9 @@
 
 MESH = pl.DeviceIdType.MESH
 TREES = 3
-STEP_ROWS = 32
+STEP_ROWS = 16
+LAG = 2
+BATCH = 4
 
 
 class Chips:
@@ -157,8 +159,8 @@
     chips, rounds, deepest,
     owner_ref, table_ref, widths_ref, weights_ref, picks_ref, rows_ref, candidates_ref, whitening_ref,
     features_ref,
-    own, land, arrive, leave, columns, places, product, unit, fresh, cosine, mine, other, factor, total, held, params_ref, theirs,
-    send_sem, recv_sem, mine_sem, other_sem, params_sem, held_sem,
+    own, land, arrive, leave, columns, places, product, unit, fresh, cosine, mine, other, mine_last, other_last, factor, total, held, params_ref, theirs,
+    send_sem, recv_sem, mine_sem, other_sem, last_sem, params_sem, held_sem,
 ):
     row, lmk, core = lax.axis_index("row"), lax.axis_index("lmk"), lax.axis_index("bw")
     me = row * chips.lmks + lmk
@@ -208,6 +210,14 @@
             device_id_type=MESH,
         )
 
+    share_last = pltpu.make_async_remote_copy(
+        src_ref=mine_last,
+        dst_ref=other_last,
+        send_sem=last_sem.at[0],
+        recv_sem=last_sem.at[1],
+        device_id=partner,
+        device_id_type=MESH,
+    )
     params_copy = pltpu.make_async_remote_copy(
         src_ref=params_ref,
         dst_ref=theirs,
@@ -216,8 +226,7 @@
         device_id=partner,
         device_id_type=MESH,
     )
-    whole_rows = whitening_ref.shape[0]
-    whitening_copy = pltpu.make_async_copy(whitening_ref, held.at[pl.ds(0, whole_rows)], held_sem)
+    whitening_copy = pltpu.make_async_copy(whitening_ref, held, held_sem)
 
     barrier = pltpu.get_barrier_semaphore()
 
@@ -253,7 +262,19 @@
         scale = lax.rsqrt(jnp.sum(widened * widened, axis=-1, keepdims=True) + 1e-06)
         return (widened * scale).astype(jnp.bfloat16)
 
-    def gather(group):
+    def products(first_tile, last_tile):
+        def tile_of(tile, carry):
+            cols = pl.ds(pl.multiple_of(tile * 256, 256), 256)
+            product[:, cols] = jnp.dot(
+                places[...], candidates_ref[:, cols], preferred_element_type=jnp.float32
+            )
+            return carry
+
+        lax.fori_loop(first_tile, last_tile, tile_of, 0)
+
+    tiles = width // 256
+
+    def gather_start(group):
         size = places.shape[0]
         lanes = lax.broadcasted_iota(jnp.int32, (size, 128), 1)
         wanted = columns[group * size : (group + 1) * size]
@@ -261,22 +282,18 @@
             places[:, tile * 128 : (tile + 1) * 128] = jnp.where(
                 wanted == lanes + tile * 128, 1.0, 0.0
             ).astype(jnp.bfloat16)
-
-        def tile_of(tile, carry):
-            cols = pl.ds(pl.multiple_of(tile * 256, 256), 256)
-            product[:, cols] = jnp.dot(
-                places[...], candidates_ref[:, cols], preferred_element_type=jnp.float32
-            )
-            return carry
-
-        lax.fori_loop(0, width // 256, tile_of, 0)
+        products(0, tiles // 2)
+
+    def gather_end(group):
+        products(tiles // 2, tiles)
+        pieces = places.shape[0] // STEP_ROWS
 
         def piece(index, carry):
             rows = pl.ds(pl.multiple_of(index * STEP_ROWS, STEP_ROWS), STEP_ROWS)
-            own[group * (size // STEP_ROWS) + index] = normalize(product[rows])
+            own[group * pieces + index] = normalize(product[rows])
             return carry
 
-        lax.fori_loop(0, size // STEP_ROWS, piece, 0)
+        lax.fori_loop(0, pieces, piece, 0)
 
     spreads = widths_ref.shape[0]
     for s in range(spreads):
@@ -284,12 +301,13 @@
         params_ref[spreads + s : spreads + s + 1] = jnp.full((1, 128), weights_ref[s], jnp.float32)
 
     groups = own.shape[0] * STEP_ROWS // places.shape[0]
-    gather(0)
+    gather_start(0)
+    gather_end(0)
     pl.semaphore_wait(barrier, chips.degree(lmk) + 1)
     params_copy.start()
 
     def pass_on(block, step, first=False, last=False):
-        slot, before = step % 2, (step + 1) % 2
+        slot, before = step % (2 * LAG), (step + LAG) % (2 * LAG)
         if not first:
             each_link(lambda link: incoming(block, before, link).wait_recv())
         values = []
@@ -307,7 +325,7 @@
         def send(link):
             if not first:
 
-                @pl.when(step >= 2)
+                @pl.when(step >= 2 * LAG)
                 def _():
                     outgoing(block, slot, link).wait_send()
 
@@ -318,123 +336,186 @@
 
         each_link(send)
 
-    def kernel_step(step):
+    lag_of = [[LAG * depth(block, tree) for tree in range(TREES)] for block in range(blocks)]
+    batches = steps // BATCH
+    rest = half - batches * BATCH * span
+    padded = cosine.shape[1]
+
+    def cosines(batch):
         for block in range(blocks):
-            for tree in range(TREES):
-                fresh[pl.ds(block * span + tree * STEP_ROWS, STEP_ROWS)] = land[
-                    block, tree, step + depth(block, tree)
-                ]
+            for piece in range(BATCH * TREES):
+                chunk, tree = batch * BATCH + piece // TREES, piece % TREES
+                to = (block * BATCH * TREES + piece) * STEP_ROWS
+                fresh[to : to + STEP_ROWS] = land[block, tree, chunk + lag_of[block][tree]]
         cosine[...] = lax.dot_general(
             unit[...], fresh[...], (((1,), (1,)), ((), ())), preferred_element_type=jnp.float32
         )
+
+    def cosines_last():
+        for block in range(blocks):
+            for piece in range(rest // STEP_ROWS):
+                chunk, tree = batches * BATCH + piece // TREES, piece % TREES
+                to = block * rest + piece * STEP_ROWS
+                fresh[to : to + STEP_ROWS] = land[block, tree, chunk + lag_of[block][tree]]
+        cosine[:, : blocks * rest] = lax.dot_general(
+            unit[...], fresh[: blocks * rest], (((1,), (1,)), ((), ())), preferred_element_type=jnp.float32
+        )
+
+    def strips(store, lanes, start, stop):
         pairs = [
-            [jnp.concatenate([ref[at : at + 1]] * (cosine.shape[1] // 128), axis=1) for at in (s, s + spreads)]
+            [jnp.concatenate([ref[at : at + 1]] * (lanes // 128), axis=1) for at in (s, s + spreads)]
             for ref in (params_ref, theirs)
             for s in range(spreads)
         ]
 
         def strip(index, carry):
-            rows = pl.ds(pl.multiple_of(index * 32, 32), 32)
-            value = cosine[rows]
+            rows = pl.ds(pl.multiple_of(index * 16, 16), 16)
+            value = cosine[rows, :lanes]
             running = jnp.zeros_like(value)
             for width_of, weight_of in pairs:
                 running = running + weight_of * jnp.exp2(width_of * value)
-            mine[step, rows] = running.astype(jnp.bfloat16)
+            store(rows, running.astype(jnp.bfloat16))
             return carry
 
-        lax.fori_loop(0, row_count // 32, strip, 0)
-        share(step).start()
-
-    def factor_rows(at, step, side):
+        lax.fori_loop(start // 16, stop // 16, strip, 0)
+
+    def strips_of(batch, start, stop):
+        def store(rows, value):
+            mine[batch, rows] = value
+
+        strips(store, padded, start, stop)
+
+    def strips_last():
+        def store(rows, value):
+            mine_last[rows] = value
+
+        strips(store, blocks * rest, 0, row_count)
+
+    def factor_rows(at, batch, side, count):
         for block in range(blocks):
-            for tree in range(TREES):
-                start = block * block_rows + side * half + step * span + tree * STEP_ROWS
-                value = held[pl.ds(pl.multiple_of(start, STEP_ROWS), STEP_ROWS)]
-                if (steps - 1) * span + tree * STEP_ROWS >= half:
-                    value = lax.select(step < steps - 1, value, jnp.zeros_like(value))
-                to = at + block * span + tree * STEP_ROWS
-                factor[to : to + STEP_ROWS] = value
-
-    def feature_step(left):
+            start = block * block_rows + side * half + batch * BATCH * span
+            value = held[pl.ds(pl.multiple_of(start, STEP_ROWS), count)]
+            factor[at + block * count : at + (block + 1) * count] = value
+
+    def features_part(left, start, stop):
         def tile_of(tile, carry):
             cols = pl.ds(pl.multiple_of(tile * 512, 512), 512)
             total[:, cols] += jnp.dot(
-                left, factor[: left.shape[1], cols], preferred_element_type=jnp.float32
+                left(), factor[:depth_of_left, cols], preferred_element_type=jnp.float32
             )
             return carry
 
-        lax.fori_loop(0, feature_count // 512, tile_of, 0)
+        depth_of_left = 2 * padded
+        lax.fori_loop(start, stop, tile_of, 0)
+
+    feature_tiles = feature_count // 512
+
+    def factors(batch):
+        factor_rows(0, batch, core, BATCH * span)
+        factor_rows(padded, jnp.maximum(batch - 1, 0), 1 - core, BATCH * span)
+
+    def features_of(batch, start, stop):
+        features_part(lambda: jnp.concatenate([mine[batch], other[batch]], axis=1), start, stop)
 
     def unit_piece(index, carry):
         rows = pl.ds(pl.multiple_of(index * 32, 32), 32)
         unit[rows] = normalize(rows_ref[rows].astype(jnp.float32))
         return carry
 
-    pass_on(0, 0, first=True)
-    pass_on(1, 0, first=True)
-    for group in range(1, groups - 1):
-        gather(group)
-    pass_on(0, 1)
-    gather(groups - 1)
-    pass_on(1, 1)
-    pass_on(0, 2)
-    lax.fori_loop(0, row_count // 32, unit_piece, 0)
-    fresh[...] = jnp.zeros_like(fresh)
-    pass_on(1, 2)
-    factor[...] = jnp.zeros_like(factor)
-    total[...] = jnp.zeros_like(total)
-    other[0] = jnp.zeros_like(other[0])
+    for step in range(LAG):
+        for block in range(blocks):
+            pass_on(block, step, first=True)
+    work_from = LAG * deepest + BATCH
+
+    def early(step, carry):
+        for block in range(blocks):
+            pass_on(block, step)
+        for group in range(1, groups):
+            pl.when(step == 2 * group)(functools.partial(gather_start, group))
+            pl.when(step == 2 * group + 1)(functools.partial(gather_end, group))
+
+        @pl.when(step == 2 * groups)
+        def _():
+            lax.fori_loop(0, row_count // 32, unit_piece, 0)
+
+        @pl.when(step == 2 * groups + 1)
+        def _():
+            total[...] = jnp.zeros_like(total)
+            other[0] = jnp.zeros_like(other[0])
+
+        return carry
+
+    lax.fori_loop(LAG, work_from, early, 0)
     params_copy.wait()
-
-    def early(step, carry):
-        pass_on(0, step)
-        pass_on(1, step)
+    whitening_copy.wait()
+
+    def middle(step, carry):
+        for block in range(blocks):
+            pass_on(block, step)
+        batch, part = (step - work_from) // BATCH, (step - work_from) % BATCH
+
+        @pl.when(part == 0)
+        def _():
+            cosines(batch)
+            strips_of(batch, 0, row_count // 3)
+
+        @pl.when(part == 1)
+        def _():
+            strips_of(batch, row_count // 3, row_count)
+            share(batch).start()
+
+        @pl.when(part == 2)
+        def _():
+            pl.when(batch >= 1)(lambda: share(batch - 1).wait_recv())
+            factors(batch)
+            features_of(batch, 0, feature_tiles // 2)
+
+        @pl.when(part == 3)
+        def _():
+            features_of(batch, feature_tiles // 2, feature_tiles)
+
         return carry
 
-    lax.fori_loop(3, deepest, early, 0)
-    whitening_copy.wait()
-    padded = mine.shape[2]
-
-    def features_of(step):
-        @pl.when(step >= 1)
-        def _():
-            share(step - 1).wait_recv()
-
-        factor_rows(0, step, core)
-        factor_rows(padded, jnp.maximum(step - 1, 0), 1 - core)
-        feature_step(jnp.concatenate([mine[step], other[step]], axis=1))
-
-    pass_on(0, deepest)
-    pass_on(1, deepest)
-    kernel_step(0)
-
-    def middle(step, carry):
-        pass_on(0, step)
-        features_of(step - deepest - 1)
-        pass_on(1, step)
-        kernel_step(step - deepest)
+    lax.fori_loop(work_from, rounds - LAG, middle, 0)
+    final = batches - 1
+    for block in range(blocks):
+        pass_on(block, rounds - 2, last=True)
+    cosines(final)
+    strips_of(final, 0, row_count)
+    share(final).start()
+    for block in range(blocks):
+        pass_on(block, rounds - 1, last=True)
+    cosines_last()
+    strips_last()
+    share_last.start()
+    share(final - 1).wait_recv()
+    factors(final)
+    features_of(final, 0, feature_tiles)
+    factor_rows(0, final, 1 - core, BATCH * span)
+    factor_rows(padded, batches, core, rest)
+    factor_rows(padded + blocks * rest, batches, 1 - core, rest)
+    share(final).wait_recv()
+    share_last.wait_recv()
+
+    def end_tile(tile, carry):
+        cols = pl.ds(pl.multiple_of(tile * 512, 512), 512)
+        left = jnp.concatenate([other[batches], mine_last[...], other_last[...]], axis=1)
+        added = jnp.dot(left, factor[: padded + 2 * blocks * rest, cols], preferred_element_type=jnp.float32)
+        features_ref[:, cols] = (total[:, cols] + added).astype(jnp.bfloat16)
         return carry
 
-    lax.fori_loop(deepest + 1, rounds - 1, middle, 0)
-    pass_on(0, rounds - 1, last=True)
-    features_of(steps - 2)
-    pass_on(1, rounds - 1, last=True)
-    kernel_step(steps - 1)
-    features_of(steps - 1)
-    share(steps - 1).wait_recv()
-    factor_rows(0, steps - 1, 1 - core)
-    feature_step(other[steps])
-    features_ref[...] = total[...].astype(jnp.bfloat16)
+    lax.fori_loop(0, feature_tiles, end_tile, 0)
+    share_last.wait_send()
 
     for block in range(blocks):
-        for slot in range(2):
+        for slot in range(2 * LAG):
             each_link(lambda link: outgoing(block, slot, link).wait_send())
 
     def sent(step, carry):
         share(step).wait_send()
         return carry
 
-    lax.fori_loop(0, steps, sent, 0)
+    lax.fori_loop(0, batches, sent, 0)
 
 
 def per_device(
@@ -448,9 +529,12 @@
     steps = -(-half // span)
     parent_link, depth, leaving = routes(chips.rows, chips.lmks)
     deepest = int(depth.max())
-    rounds = steps + deepest
-    padded = -(-blocks * span // 128) * 128
-    group_rows = 4 * span
+    rounds = steps + LAG * deepest
+    batches = steps // BATCH
+    rest = half - batches * BATCH * span
+    assert steps == batches * BATCH + LAG and rest % 16 == 0
+    padded = blocks * BATCH * span
+    group_rows = 8 * span
     own_rows = -(-half // group_rows) * group_rows
 
     first = sum((parent_link[..., t] + 1) << (3 * t) for t in range(TREES))
@@ -458,7 +542,7 @@
     second = sum(leaving[..., link] << (2 * link) for link in range(chips.links))
     table = np.stack([first, second], axis=-1).reshape(-1).astype(np.int32)
 
-    slots = (blocks, 2, chips.links)
+    slots = (blocks, 2 * LAG, chips.links)
     bf16, f32 = jnp.bfloat16, jnp.float32
     in_vmem = pl.BlockSpec(memory_space=pltpu.VMEM)
     in_smem = pl.BlockSpec(memory_space=pltpu.SMEM)
@@ -478,17 +562,20 @@
             pltpu.VMEM((row_count, width), bf16),
             pltpu.VMEM((padded, width), bf16),
             pltpu.VMEM((row_count, padded), f32),
-            pltpu.VMEM((steps, row_count, padded), bf16),
-            pltpu.VMEM((steps + 1, row_count, padded), bf16),
+            pltpu.VMEM((batches, row_count, padded), bf16),
+            pltpu.VMEM((batches + 1, row_count, padded), bf16),
+            pltpu.VMEM((row_count, blocks * rest), bf16),
+            pltpu.VMEM((row_count, blocks * rest), bf16),
             pltpu.VMEM((2 * padded, feature_count), bf16),
             pltpu.VMEM((row_count, feature_count), f32),
-            pltpu.VMEM((whitening.shape[0] + STEP_ROWS, feature_count), bf16),
+            pltpu.VMEM(whitening.shape, bf16),
             pltpu.VMEM((2 * inverse_width.shape[0], 128), f32),
             pltpu.VMEM((2 * inverse_width.shape[0], 128), f32),
             pltpu.SemaphoreType.DMA(slots),
             pltpu.SemaphoreType.DMA(slots),
-            pltpu.SemaphoreType.DMA((steps,)),
-            pltpu.SemaphoreType.DMA((steps,)),
+            pltpu.SemaphoreType.DMA((batches,)),
+            pltpu.SemaphoreType.DMA((batches,)),
+            pltpu.SemaphoreType.DMA((2,)),
             pltpu.SemaphoreType.DMA((2,)),
             pltpu.SemaphoreType.DMA,
         ],

time: 83.5 us -> 81.1 us (0.971)
  Pallas kernels: 80.6 us -> 78.2 us
    pallas_call x1, Pallas kernels: 80.6 us -> 78.2 us  [per_device(): pl.pallas_call(functools.partial(fused, chips, rounds, deepest), out_shap...]
where the time goes in v4:
time: 81.1 us; the launch traced here: 80.9 us
  Pallas kernels  78.2 us (96%)
  local copies, waits for them, and re-layouts  2.73 us (3%)
    pallas_call x1, Pallas kernels, per_device(): pl.pallas_call(functools.partial(fused, chips, rounds, deepest), out_shap...  78.2 us
    unnamed x1, local copies, waits for them, and re-layouts  2.73 us

profile of v4, /device:TPU:0, one launch (start us, length us, event | category | flops | bytes accessed | tf_op | source)
XLA Modules:
  0.0 80.9 jit_solution(9808732273375719048)
XLA Ops:
  0.0 78.2 %fused.1 = bf16[384,2048]{1,0:T(8,128)(2,1)} custom-call(s32[2]{0:T(128)} %owner_ref.1, s32[512]{0:T(512)} %constant.2.clone.table_ref, f32[4]{0:T(128)} %widths_ref.1, f32[4]{0:T(128)} %weights_ref.1, s32[2,2048]{1,0:T(2,128)} %picks_ref.1, bf16[384,1024]{1,0:T(8,128)(2,1)} %rows_ref.1, bf16[2048,1024]{1,0:T(8,128)(2,1)} %candidates_ref.1, ...), custom_call_target="tpu_custom_call" | custom-call | tf_op jit(solution)/shard_map/fused/pallas_call | solution.py:549
  78.2 2.7 %copy.10 = bf16[384,2048]{1,0:T(8,128)(2,1)} copy(bf16[384,2048]{1,0:T(8,128)(2,1)} %fused.1) | data formatting | bytes 3145728

commit v5 on v4

--- a/solution.py
+++ b/solution.py
@@ -133,7 +133,7 @@
     n = chips.count
     parent_link = np.full((n, n, TREES), -1, np.int32)
     depth = np.zeros((n, n, TREES), np.int32)
-    leaving = np.zeros((n, n, chips.links), np.int32)
+    leaving = np.full((n, n, chips.links), 3, np.int32)
     for owner in range(n):
         image, root = moved(chips, owner)
         for tree in range(TREES):
@@ -156,15 +156,16 @@
 
 
 def fused(
-    chips, rounds, deepest,
+    chips, rounds, deepest, fixed_words,
     owner_ref, table_ref, widths_ref, weights_ref, picks_ref, rows_ref, candidates_ref, whitening_ref,
     features_ref,
-    own, land, arrive, leave, columns, places, product, unit, fresh, cosine, mine, other, mine_last, other_last, factor, total, held, params_ref, theirs,
-    send_sem, recv_sem, mine_sem, other_sem, last_sem, params_sem, held_sem,
+    own, fixed, land, arrive, leave, columns, places, product, unit, fresh, cosine, mine, other, mine_last, other_last, factor, total, held, params_ref, theirs,
+    fixed_send_sem, fixed_sem, send_sem, recv_sem, mine_sem, other_sem, last_sem, params_sem, held_sem,
 ):
     row, lmk, core = lax.axis_index("row"), lax.axis_index("lmk"), lax.axis_index("bw")
     me = row * chips.lmks + lmk
     blocks = owner_ref.shape[0]
+    last_chip = chips.count - 1
     block_rows, width = candidates_ref.shape
     half = block_rows // 2
     row_count, feature_count = total.shape
@@ -184,21 +185,31 @@
         r, k = chips.neighbour(link, row, lmk)
         return {"row": r, "lmk": k}
 
-    def copy_to(link, block, slot, arriving):
+    def copy_to(link, slot, arriving):
         return pltpu.make_async_remote_copy(
-            src_ref=leave.at[block, slot, link],
-            dst_ref=arrive.at[block, slot, arriving],
-            send_sem=send_sem.at[block, slot, link],
-            recv_sem=recv_sem.at[block, slot, arriving],
+            src_ref=leave.at[slot, link],
+            dst_ref=arrive.at[slot, arriving],
+            send_sem=send_sem.at[slot, link],
+            recv_sem=recv_sem.at[slot, arriving],
             device_id=target(link),
             device_id_type=MESH,
         )
 
-    def outgoing(block, slot, link):
-        return copy_to(link, block, slot, chips.back[link])
-
-    def incoming(block, slot, link):
-        return copy_to(link, block, slot, link)
+    def outgoing(slot, link):
+        return copy_to(link, slot, chips.back[link])
+
+    def incoming(slot, link):
+        return copy_to(link, slot, link)
+
+    def fixed_copy(link, tree, chunk):
+        return pltpu.make_async_remote_copy(
+            src_ref=fixed.at[tree, chunk],
+            dst_ref=fixed.at[tree, chunk],
+            send_sem=fixed_send_sem.at[link, chunk % 4],
+            recv_sem=fixed_sem.at[tree, chunk],
+            device_id=target(link),
+            device_id_type=MESH,
+        )
 
     def share(step):
         return pltpu.make_async_remote_copy(
@@ -237,24 +248,34 @@
     pl.semaphore_signal(barrier, inc=1, device_id=partner, device_id_type=MESH)
     whitening_copy.start()
 
-    first_word, second_word = [], []
-    for block in range(blocks):
-        at = 2 * (owner_ref[block] * chips.count + me)
-        first_word.append(table_ref[at])
-        second_word.append(table_ref[at + 1])
-
-    def parent(block, tree):
-        return (first_word[block] >> (3 * tree)) & 7
-
-    def depth(block, tree):
-        return (first_word[block] >> (9 + 4 * tree)) & 15
-
-    def leaving(block, link):
-        return (second_word[block] >> (2 * link)) & 3
+    last_block = (owner_ref[1] == last_chip).astype(jnp.int32)
+    stream_block = [last_block, 1 - last_block]
+    other_owner = jnp.where(last_block == 1, owner_ref[0], owner_ref[1])
+    at = 2 * (other_owner * chips.count + me)
+    flood_words = table_ref[at], table_ref[at + 1]
+    def is_equal(a, b):
+        return 1 - jnp.minimum(jnp.maximum(a - b, b - a), 1)
+
+    place_words = [
+        sum(is_equal(me, chip) * word for chip, word in enumerate(words)) for words in fixed_words
+    ]
+
+    def parent(words, tree):
+        return (words[0] // 8**tree) % 8
+
+    def depth(words, tree):
+        return (words[0] // (512 * 16**tree)) % 16
+
+    def leaving(words, link):
+        return (words[1] // 4**link) % 4
+
+    fixed_depth = [depth(place_words, tree) for tree in range(TREES)]
+    fixed_leaving = [leaving(place_words, link) for link in range(chips.links)]
 
     for group in range(half // 128):
         lanes_of = pl.ds(pl.multiple_of(core * half + group * 128, 128), 128)
-        picked = lax.select(owner_ref[1] == me, picks_ref[1:2, lanes_of], picks_ref[0:1, lanes_of])
+        wanted_block = jnp.where(me == last_chip, stream_block[0], stream_block[1])
+        picked = lax.select(wanted_block == 1, picks_ref[1:2, lanes_of], picks_ref[0:1, lanes_of])
         columns[group * 128 : (group + 1) * 128] = jnp.transpose(jnp.broadcast_to(picked, (128, 128)))
     columns[half:] = jnp.zeros_like(columns[half:])
 
@@ -306,18 +327,44 @@
     pl.semaphore_wait(barrier, chips.degree(lmk) + 1)
     params_copy.start()
 
-    def pass_on(block, step, first=False, last=False):
+    def relay(step):
+        for tree in range(TREES):
+            chunk = step - LAG * fixed_depth[tree]
+            live = jnp.logical_and(chunk >= 0, chunk < steps)
+
+            @pl.when(jnp.logical_and(live, me == last_chip))
+            def _():
+                fixed[tree, chunk] = own[chunk * TREES + tree]
+
+            @pl.when(jnp.logical_and(live, me != last_chip))
+            def _():
+                fixed_copy(0, tree, chunk).wait_recv()
+
+        for link in range(chips.links):
+            tree = fixed_leaving[link]
+            chunk = step - LAG * sum(is_equal(tree, t) * fixed_depth[t] for t in range(TREES))
+            live = jnp.logical_and(chunk >= 0, chunk < steps)
+
+            @pl.when(jnp.logical_and(live, tree < TREES))
+            def _():
+                @pl.when(chunk >= 4)
+                def _():
+                    fixed_copy(link, tree, chunk).wait_send()
+
+                fixed_copy(link, tree, chunk).start()
+
+    def pass_on(step, first=False, last=False):
         slot, before = step % (2 * LAG), (step + LAG) % (2 * LAG)
         if not first:
-            each_link(lambda link: incoming(block, before, link).wait_recv())
+            each_link(lambda link: incoming(before, link).wait_recv())
         values = []
         for tree in range(TREES):
-            origin = parent(block, tree)
+            origin = parent(flood_words, tree)
             value = own[jnp.minimum(step, steps - 1) * TREES + tree]
             if not first:
                 for link in range(chips.links):
-                    value = lax.select(origin == link + 1, arrive[block, before, link], value)
-            land[block, tree, step] = value
+                    value = lax.select(origin == link + 1, arrive[before, link], value)
+            land[tree, step] = value
             values.append(value)
         if last:
             return
@@ -327,16 +374,24 @@
 
                 @pl.when(step >= 2 * LAG)
                 def _():
-                    outgoing(block, slot, link).wait_send()
-
-            tree = leaving(block, link)
+                    outgoing(slot, link).wait_send()
+
+            tree = leaving(flood_words, link)
             value = lax.select(tree == 1, values[1], values[0])
-            leave[block, slot, link] = lax.select(tree == 2, values[2], value)
-            outgoing(block, slot, link).start()
+            leave[slot, link] = lax.select(tree == 2, values[2], value)
+            outgoing(slot, link).start()
 
         each_link(send)
 
-    lag_of = [[LAG * depth(block, tree) for tree in range(TREES)] for block in range(blocks)]
+    def one_round(step, first=False, last=False):
+        relay(step)
+        pass_on(step, first, last)
+
+    lag_of = [LAG * depth(flood_words, tree) for tree in range(TREES)]
+
+    def landed(stream, tree, chunk):
+        return fixed[tree, chunk] if stream == 0 else land[tree, chunk + lag_of[tree]]
+
     batches = steps // BATCH
     rest = half - batches * BATCH * span
     padded = cosine.shape[1]
@@ -346,7 +401,7 @@
             for piece in range(BATCH * TREES):
                 chunk, tree = batch * BATCH + piece // TREES, piece % TREES
                 to = (block * BATCH * TREES + piece) * STEP_ROWS
-                fresh[to : to + STEP_ROWS] = land[block, tree, chunk + lag_of[block][tree]]
+                fresh[to : to + STEP_ROWS] = landed(block, tree, chunk)
         cosine[...] = lax.dot_general(
             unit[...], fresh[...], (((1,), (1,)), ((), ())), preferred_element_type=jnp.float32
         )
@@ -356,7 +411,7 @@
             for piece in range(rest // STEP_ROWS):
                 chunk, tree = batches * BATCH + piece // TREES, piece % TREES
                 to = block * rest + piece * STEP_ROWS
-                fresh[to : to + STEP_ROWS] = land[block, tree, chunk + lag_of[block][tree]]
+                fresh[to : to + STEP_ROWS] = landed(block, tree, chunk)
         cosine[:, : blocks * rest] = lax.dot_general(
             unit[...], fresh[: blocks * rest], (((1,), (1,)), ((), ())), preferred_element_type=jnp.float32
         )
@@ -393,8 +448,12 @@
 
     def factor_rows(at, batch, side, count):
         for block in range(blocks):
-            start = block * block_rows + side * half + batch * BATCH * span
-            value = held[pl.ds(pl.multiple_of(start, STEP_ROWS), count)]
+            start = side * half + batch * BATCH * span
+            value = lax.select(
+                stream_block[block] == 1,
+                held[pl.ds(pl.multiple_of(start + block_rows, STEP_ROWS), count)],
+                held[pl.ds(pl.multiple_of(start, STEP_ROWS), count)],
+            )
             factor[at + block * count : at + (block + 1) * count] = value
 
     def features_part(left, start, stop):
@@ -423,13 +482,11 @@
         return carry
 
     for step in range(LAG):
-        for block in range(blocks):
-            pass_on(block, step, first=True)
+        one_round(step, first=True)
     work_from = LAG * deepest + BATCH
 
     def early(step, carry):
-        for block in range(blocks):
-            pass_on(block, step)
+        one_round(step)
         for group in range(1, groups):
             pl.when(step == 2 * group)(functools.partial(gather_start, group))
             pl.when(step == 2 * group + 1)(functools.partial(gather_end, group))
@@ -450,8 +507,7 @@
     whitening_copy.wait()
 
     def middle(step, carry):
-        for block in range(blocks):
-            pass_on(block, step)
+        one_round(step)
         batch, part = (step - work_from) // BATCH, (step - work_from) % BATCH
 
         @pl.when(part == 0)
@@ -478,13 +534,11 @@
 
     lax.fori_loop(work_from, rounds - LAG, middle, 0)
     final = batches - 1
-    for block in range(blocks):
-        pass_on(block, rounds - 2, last=True)
+    one_round(rounds - 2, last=True)
     cosines(final)
     strips_of(final, 0, row_count)
     share(final).start()
-    for block in range(blocks):
-        pass_on(block, rounds - 1, last=True)
+    one_round(rounds - 1, last=True)
     cosines_last()
     strips_last()
     share_last.start()
@@ -507,9 +561,14 @@
     lax.fori_loop(0, feature_tiles, end_tile, 0)
     share_last.wait_send()
 
-    for block in range(blocks):
-        for slot in range(2 * LAG):
-            each_link(lambda link: outgoing(block, slot, link).wait_send())
+    for slot in range(2 * LAG):
+        each_link(lambda link: outgoing(slot, link).wait_send())
+    for link in range(chips.links):
+
+        @pl.when(fixed_leaving[link] < TREES)
+        def _():
+            for chunk in range(steps - 4, steps):
+                fixed_copy(link, fixed_leaving[link], chunk).wait_send()
 
     def sent(step, carry):
         share(step).wait_send()
@@ -541,19 +600,21 @@
     first = first + sum(depth[..., t] << (9 + 4 * t) for t in range(TREES))
     second = sum(leaving[..., link] << (2 * link) for link in range(chips.links))
     table = np.stack([first, second], axis=-1).reshape(-1).astype(np.int32)
-
-    slots = (blocks, 2 * LAG, chips.links)
+    fixed_words = [[int(word) for word in words[chips.count - 1]] for words in (first, second)]
+
+    slots = (2 * LAG, chips.links)
     bf16, f32 = jnp.bfloat16, jnp.float32
     in_vmem = pl.BlockSpec(memory_space=pltpu.VMEM)
     in_smem = pl.BlockSpec(memory_space=pltpu.SMEM)
     return pl.pallas_call(
-        functools.partial(fused, chips, rounds, deepest),
+        functools.partial(fused, chips, rounds, deepest, fixed_words),
         out_shape=jax.ShapeDtypeStruct((row_count, feature_count), bf16),
         in_specs=[in_smem] * 4 + [in_vmem] * 3 + [pl.BlockSpec(memory_space=pl.ANY)],
         out_specs=in_vmem,
         scratch_shapes=[
             pltpu.VMEM((own_rows // STEP_ROWS, STEP_ROWS, width), bf16),
-            pltpu.VMEM((blocks, TREES, rounds, STEP_ROWS, width), bf16),
+            pltpu.VMEM((TREES, steps, STEP_ROWS, width), bf16),
+            pltpu.VMEM((TREES, rounds, STEP_ROWS, width), bf16),
             pltpu.VMEM(slots + (STEP_ROWS, width), bf16),
             pltpu.VMEM(slots + (STEP_ROWS, width), bf16),
             pltpu.VMEM((own_rows, 128), jnp.int32),
@@ -571,6 +632,8 @@
             pltpu.VMEM(whitening.shape, bf16),
             pltpu.VMEM((2 * inverse_width.shape[0], 128), f32),
             pltpu.VMEM((2 * inverse_width.shape[0], 128), f32),
+            pltpu.SemaphoreType.DMA((chips.links, 4)),
+            pltpu.SemaphoreType.DMA((TREES, steps)),
             pltpu.SemaphoreType.DMA(slots),
             pltpu.SemaphoreType.DMA(slots),
             pltpu.SemaphoreType.DMA((batches,)),

time: 81.1 us -> 82.2 us (1.014)
  Pallas kernels: 78.2 us -> 79.4 us
    pallas_call x1, Pallas kernels: 78.2 us -> 79.4 us  [per_device(): pl.pallas_call(functools.partial(fused, chips, rounds, deepest, fixed_wor...]
where the time goes in v5:
time: 82.2 us; the launch traced here: 82.1 us
  Pallas kernels  79.4 us (97%)
  local copies, waits for them, and re-layouts  2.73 us (3%)
    pallas_call x1, Pallas kernels, per_device(): pl.pallas_call(functools.partial(fused, chips, rounds, deepest, fixed_wor...  79.4 us
    unnamed x1, local copies, waits for them, and re-layouts  2.73 us

profile of v5, /device:TPU:0, one launch (start us, length us, event | category | flops | bytes accessed | tf_op | source)
XLA Modules:
  0.0 82.1 jit_solution(11446501324413014547)
XLA Ops:
  0.0 79.4 %fused.1 = bf16[384,2048]{1,0:T(8,128)(2,1)} custom-call(s32[2]{0:T(128)} %owner_ref.1, s32[512]{0:T(512)} %constant.2.clone.table_ref, f32[4]{0:T(128)} %widths_ref.1, f32[4]{0:T(128)} %weights_ref.1, s32[2,2048]{1,0:T(2,128)} %picks_ref.1, bf16[384,1024]{1,0:T(8,128)(2,1)} %rows_ref.1, bf16[2048,1024]{1,0:T(8,128)(2,1)} %candidates_ref.1, ...), custom_call_target="tpu_custom_call" | custom-call | tf_op jit(solution)/shard_map/fused/pallas_call | solution.py:609
  79.4 2.7 %copy.10 = bf16[384,2048]{1,0:T(8,128)(2,1)} copy(bf16[384,2048]{1,0:T(8,128)(2,1)} %fused.1) | data formatting | bytes 3145728
